TPU v7x, 32 devices: a whole 2x2x4 slice. The times are simulated.
32 devices in a mesh: case: 2 (over y), lon: 4 (over z), lat: 2 (over x), sub: 2 (over core).
Axes of the slice: x: 2, y: 2, z: 4, core: 2. Of those that a mesh axis runs over, the one named last changes fastest.
Arguments:
- traj_u: float32 [6, 128, 2048], P('case', ('lat', 'sub'), 'lon'), parts along dimension 0, may hold values from -4 to 4
- traj_v: float32 [6, 128, 2048], P('case', ('lat', 'sub'), 'lon'), parts along dimension 0, may hold values from -4 to 4
- adj_h: float32 [16, 128, 2048], P('case', ('lat', 'sub'), 'lon'), parts along dimension 0, may hold values from -6 to 6
- adj_u: float32 [16, 128, 2048], P('case', ('lat', 'sub'), 'lon'), parts along dimension 0, may hold values from -6 to 6
- adj_v: float32 [16, 128, 2048], P('case', ('lat', 'sub'), 'lon'), parts along dimension 0, may hold values from -6 to 6
- depth: float32 [128, 2048], P(('lat', 'sub'), 'lon'), may hold values from 0.25 to 1
- drag: float32 [128, 2048], P(('lat', 'sub'), 'lon'), may hold values from 0.1 to 1
- land: int32 [128, 2048], P(('lat', 'sub'), 'lon'), may hold values 0 or 1
- wet_u: int32 [6, 128, 2048], P('case', ('lat', 'sub'), 'lon'), parts along dimension 0, may hold values 0 or 1
- wet_v: int32 [6, 128, 2048], P('case', ('lat', 'sub'), 'lon'), parts along dimension 0, may hold values 0 or 1
Outputs:
- out_h: float32 [16, 128, 2048], P('case', ('lat', 'sub'), 'lon'), parts along dimension 0
- out_u: float32 [16, 128, 2048], P('case', ('lat', 'sub'), 'lon'), parts along dimension 0
- out_v: float32 [16, 128, 2048], P('case', ('lat', 'sub'), 'lon'), parts along dimension 0
- out_depth: float32 [16, 128, 2048], P('case', ('lat', 'sub'), 'lon'), parts along dimension 0
- out_drag: float32 [16, 128, 2048], P('case', ('lat', 'sub'), 'lon'), parts along dimension 0
There are 2 independent parts, one for each index of `case`. A program takes and returns all parts, laid end to end along the dimension named above; an argument that names none is the same for every part. Nothing has to cross between parts.
All inputs are finite; a program needn't handle non-finite values. No bound on the sum of `land` or of `wet_u` or of `wet_v` on one device may be relied on, other than what follows from the above.
Results may differ from a plain program's by a relative error of at most 0.00002.
Values sent between devices are 32-bit elements; how exact they have to be, the bound alone decides.
No kernel may reach another device: no remote copies, remote signals or barrier semaphores. Data moves between devices by JAX's collectives and lax.ppermute only.
A program may use at most 64 MiB of HBM per device.

v0:
```python
import functools

import jax
import jax.numpy as jnp
from jax import lax
from jax.experimental import pallas as pl
from jax.experimental.pallas import tpu as pltpu
from jax.sharding import PartitionSpec as P

time_step = 0.5
gravity = 1.0
speed_floor = 0.01

ROWS = ("lat", "sub")
GRID = ("lon", "lat", "sub")
TILE = 8
LANES = 128
DEEP = 4
GROUP = 16
PAIR = 4
VMEM_LIMIT = 48 * 1024 * 1024


def iota(shape, axis):
    return lax.broadcasted_iota(jnp.int32, shape, axis)


def place():
    row = lax.axis_index("lat") * lax.axis_size("sub") + lax.axis_index("sub")
    last = lax.axis_size("lat") * lax.axis_size("sub") - 1
    return row % 2 == 0, row == last, row == 0


STATE_SLOTS = (3, 3, 4)
SHARED = (
    (("traj_v", 2), 2, 3, True),
    (("traj_v", 1), 2, 2, True),
    (("traj_v", 0), 2, 1, True),
    (("traj_u", 2), 1, 2, True),
    (("traj_u", 1), 1, 1, True),
    (("wet_v", 1), 2, 3, False),
    (("wet_v", 0), 2, 2, False),
    (("wet_u", 1), 1, 2, False),
    (("wet_u", 0), 1, 1, False),
    (("depth", None), 0, 3, False),
    (("drag", None), 3, 3, False),
    (("land", None), 0, 3, False),
)
NAMES = ("adj_h", "adj_u", "adj_v", "traj_u", "traj_v", "wet_u", "wet_v", "depth", "drag", "land")
TILES = tuple(entry[0] for entry in SHARED[:10]) + (("drag", 1), ("drag", 2), ("land", None), ("traj_u", 0))


def load(refs, name, step):
    value = refs[name][...] if step is None or name == "drag" else refs[name][step]
    return value.astype(jnp.float32)


def message_rows(count):
    rows = sum(STATE_SLOTS) * count + sum(entry[2] for entry in SHARED)
    return -(-rows // TILE) * TILE


def row_plan(count):
    plan, at = [], 0
    for sens in range(count):
        for kind in range(3):
            plan.append(((NAMES[kind], sens), kind, kind > 0, at, STATE_SLOTS[kind]))
            at += STATE_SLOTS[kind]
    for key, kind, slots, turned in SHARED:
        plan.append((key, kind, turned, at, slots))
        at += slots
    return plan


def lane_tiles(value):
    return [value[:, at : at + LANES] for at in range(0, value.shape[1], LANES)]


def masked(refs, key):
    name, step = key
    value = load(refs, name, step)
    if name == "adj_u":
        value = value * load(refs, "wet_u", 2)
    if name == "adj_v":
        value = value * load(refs, "wet_v", 2)
    return value


def start_copies(arrays, held, sems, window, names=NAMES):
    copies = {}
    for number, name in enumerate(NAMES):
        array = arrays[name]
        if name in names:
            lead = (slice(None),) * (array.ndim - 2)
            source = array.at[lead + window(*array.shape[-2:])]
            copies[name] = pltpu.make_async_copy(source, held[name], sems.at[number])
            copies[name].start()
    return copies


def edge(held, rows):
    return {name: ref.at[(slice(None),) * (ref.ndim - 2) + (rows,)] for name, ref in held.items()}


def pack_edges(*refs):
    arrays = dict(zip(NAMES, refs[:10]))
    held = dict(zip(NAMES, refs[10:20]))
    near, target, sems = refs[20:23]
    even, at_top, _ = place()
    count, rows, width = arrays["adj_h"].shape
    for copy in start_copies(arrays, held, sems, lambda rows, width: (slice(None), slice(None))).values():
        copy.wait()
    low, held = edge(held, pl.ds(0, TILE)), edge(held, pl.ds(rows - TILE, TILE))
    for key, kind, turned, at, slots in row_plan(count):
        here = slice(at, at + slots)
        south, north = masked(low, key)[:slots], masked(held, key)[TILE - slots :]
        near[here, :] = jnp.where(even, north, south)
        target[here, :] = jnp.where(even, south, north)

    @pl.when(at_top)
    def _():
        row = iota((TILE, LANES), 0)
        lane = LANES - 1 - iota((TILE, LANES), 1)
        for key, kind, turned, at, slots in row_plan(count):
            value = masked(held, key)
            sources = [TILE - 1 - slot for slot in range(slots)]
            if kind == 2:
                sources = [TILE - 2 - slot for slot in range(slots - 1)] + [TILE - 1]
            order = jnp.zeros((TILE, LANES), jnp.int32)
            for slot, source in enumerate(sources):
                order = jnp.where(row == slot, source, order)
            pieces = []
            for piece in lane_tiles(value)[::-1]:
                piece = jnp.take_along_axis(piece, lane, axis=1)
                piece = jnp.take_along_axis(piece, order, axis=0)
                if turned:
                    piece = jnp.where(row == slots - 1, piece, -piece) if kind == 2 else -piece
                pieces.append(piece)
            target[at : at + slots, :] = jnp.concatenate(pieces, axis=1)[:slots]


def group_lanes(field, count):
    if field < 3 * count:
        return 0, GROUP * (field // 3) + DEEP * (field % 3)
    static = field - 3 * count
    return static // count, GROUP * (static % count) + 3 * DEEP


def column_fields(count):
    keys = [(NAMES[kind], sens) for sens in range(count) for kind in range(3)] + list(TILES)
    fields = [(key,) + group_lanes(field, count) + (field,) for field, key in enumerate(keys)]
    return sorted(fields, key=lambda entry: entry[1:])


def pack_columns(held, to_west, to_east):
    count, rows, width = held["adj_h"].shape
    lane = iota((rows, LANES), 1)
    for target, first, origin in ((to_west, 0, 0), (to_east, width - LANES, LANES - DEEP)):
        side_held = {name: ref.at[(slice(None),) * (ref.ndim - 1) + (pl.ds(first, LANES),)] for name, ref in held.items()}
        packed = [None, None]
        for key, side, at, _ in column_fields(count):
            value = masked(side_held, key)
            shift = (at - origin) % LANES
            if shift:
                value = pltpu.roll(value, shift, 1)
            packed[side] = value if packed[side] is None else jnp.where(lane >= at, value, packed[side])
        for side in range(2):
            target[:, side * LANES : (side + 1) * LANES] = packed[side]


def merge_rows(one, two, own_west, own_east, halo, halo_static, inner, outer):
    even, at_top, at_bottom = place()
    width = one.shape[1]
    rows = own_west.shape[0]
    count = halo.shape[0] // 3
    lane = iota((TILE, LANES), 1)
    west_inner = lax.axis_index("lon") % 2 == 1
    inner[:rows, :] = jnp.where(west_inner, own_west[...], own_east[...])
    outer[:rows, :] = jnp.where(west_inner, own_east[...], own_west[...])
    field = 0
    tiles = []
    for key, kind, turned, at, slots in row_plan(count):
        here = slice(at, at + slots)
        north = jnp.where(even, one[here, :], two[here, :])
        south = jnp.where(even, two[here, :], one[here, :])
        south = jnp.where(at_bottom, 0.0, south)
        blank = jnp.zeros((DEEP - slots, width), jnp.float32)
        gap = [blank] if slots < DEEP else []
        plain = jnp.concatenate([north] + gap + gap + [south], axis=0)
        values = [plain]
        if kind >= 2 and slots < DEEP:
            fold = ([north[:-1]] if slots > 1 else []) + gap + [north[-1:]] + gap + [south]
            if kind == 3:
                fold = [north[1:], blank, north[:1]] + gap + [south]
                values.append(jnp.where(at_top, jnp.concatenate(fold, axis=0), plain))
            else:
                values = [jnp.where(at_top, jnp.concatenate(fold, axis=0), plain)]
        tiles += values
    tiles.append(jnp.zeros((TILE, width), jnp.float32))
    for field, value in enumerate(tiles):
        if field < halo.shape[0]:
            halo[field] = value
        else:
            halo_static[field - halo.shape[0]] = value
    packed = [[None, None], [None, None]]
    for key, side, start, field in column_fields(count):
        pieces = lane_tiles(tiles[field])
        for way, piece, origin in ((0, pieces[0], 0), (1, pieces[-1], LANES - DEEP)):
            shift = (start - origin) % LANES
            if shift:
                piece = pltpu.roll(piece, shift, 1)
            held = packed[way][side]
            packed[way][side] = piece if held is None else jnp.where(lane >= start, piece, held)
    for side in range(2):
        cols = slice(side * LANES, (side + 1) * LANES)
        west, east = packed[0][side], packed[1][side]
        inner[rows:, cols] = jnp.where(west_inner, west, east)
        outer[rows:, cols] = jnp.where(west_inner, east, west)


def rows_of(tile):
    return slice(tile * TILE, (tile + 1) * TILE)


KEEP, DEPTH, DRAG, VEL = 0, 2, 4, 6
FIRST, LAND, RATIO = 0, 2, 3


def coefficients(field, halo, moving, fixed):
    cells = field(("depth", None), 0)
    cells = jnp.where(cells > 0.0, cells, 1.0)
    height, wide = cells.shape
    row = iota((height, wide), 0)
    stores = [(fixed, (LAND,), 0.5 * field(("land", None), 0))]
    for side, way in enumerate("uv"):
        kind = side + 1
        if side == 0:
            face = 0.5 * (cells + pltpu.roll(cells, wide - 1, 1))
        else:
            face = 0.5 * (cells + pltpu.roll(cells, height - 1, 0))
            if halo is not None:
                face = jnp.where(row == halo * TILE + 3, pltpu.roll(face, DEEP, 0), face)
        inverse = 1.0 / face
        ratio = -field(("drag", kind), kind) * inverse
        wet = [field(("wet_" + way, step), kind) for step in range(3)]
        stores += [(fixed, (RATIO + side,), ratio), (fixed, (FIRST + side,), 0.5 * wet[2])]
        for step in range(3):
            now = field(("traj_" + way, step), kind)
            square = now * now
            speed = jnp.sqrt(square + speed_floor)
            keep = 2.0 + ratio * (speed + square / speed)
            deep = face
            if step > 0:
                mask = 0.5 * wet[step - 1]
                keep, deep = keep * mask, deep * mask
            stores += [
                (moving, (KEEP + side, step), keep),
                (moving, (DEPTH + side, step), deep),
                (moving, (DRAG + side, step), -now * speed * inverse),
                (moving, (VEL + side, step), now),
            ]
    for ref, index, value in stores:
        ref[index] = value


def south_of(values, tile):
    row = iota(values[tile].shape, 0)
    return jnp.where(row == 0, pltpu.roll(values[tile - 1], 1, 0), pltpu.roll(values[tile], 1, 0))


def north_of(values, tile):
    row = iota(values[tile].shape, 0)
    after = values[(tile + 1) % len(values)]
    return jnp.where(row == TILE - 1, pltpu.roll(after, TILE - 1, 0), pltpu.roll(values[tile], TILE - 1, 0))


def march(states, moving, fixed, halo, at_top):
    count = len(states[0][0])
    wide = states[0][0][0].shape[1]
    row = iota((TILE, wide), 0)
    group = range(len(states))

    def east_of(value):
        return pltpu.roll(value, wide - 1, 1)

    def west_of(value):
        return pltpu.roll(value, 1, 1)

    def fold_row(value):
        return jnp.where(at_top & (row == TILE - 1), pltpu.roll(value, DEEP, 0), 0.0)

    high = [list(state[0]) for state in states]
    flow_u, flow_v = [[] for _ in group], [[] for _ in group]
    for tile in range(count):
        here = rows_of(tile)
        first_u, first_v = fixed[FIRST, here, :], fixed[FIRST + 1, here, :]
        for one in group:
            flow_u[one].append(first_u * states[one][1][tile])
            flow_v[one].append(first_v * states[one][2][tile])
    history = []
    for step in (2, 1, 0):
        sea, turns_u, turns_v, next_u, next_v = ([[] for _ in group] for _ in range(5))
        face = [list(flows) for flows in flow_v]
        if halo is not None:
            for one in group:
                face[one][halo - 1] = flow_v[one][halo - 1] - fold_row(flow_v[one][halo])
        for tile in range(count):
            land = fixed[LAND, rows_of(tile), :]
            for one in group:
                high[one][tile] = (
                    high[one][tile]
                    + (flow_u[one][tile] - west_of(flow_u[one][tile]))
                    + (face[one][tile] - south_of(face[one], tile))
                )
                sea[one].append(land * high[one][tile])
        for tile in range(count):
            here = rows_of(tile)
            keep_u, keep_v = moving[KEEP, step, here, :], moving[KEEP + 1, step, here, :]
            deep_u, deep_v = moving[DEPTH, step, here, :], moving[DEPTH + 1, step, here, :]
            for one in group:
                turn_u = east_of(sea[one][tile]) - sea[one][tile]
                turn_v = north_of(sea[one], tile) - sea[one][tile]
                if tile == halo:
                    turn_v = jnp.where(row == 3, -pltpu.roll(turns_v[one][tile - 1], DEEP, 0), turn_v)
                turns_u[one].append(turn_u)
                turns_v[one].append(turn_v)
                next_u[one].append(keep_u * flow_u[one][tile] + deep_u * turn_u)
                next_v[one].append(keep_v * flow_v[one][tile] + deep_v * turn_v)
        history.append((step, flow_u, flow_v, turns_u, turns_v))
        flow_u, flow_v = next_u, next_v

    face_u, face_v, drags = ([[] for _ in group] for _ in range(3))
    for tile in range(count):
        here = rows_of(tile)
        sums = [[0.0] * 4 for _ in group]
        for step, steps_u, steps_v, turns_u, turns_v in history:
            for number, (index, values) in enumerate(
                ((DRAG, steps_u), (DRAG + 1, steps_v), (VEL, turns_u), (VEL + 1, turns_v))
            ):
                factor = moving[index, step, here, :]
                for one in group:
                    sums[one][number] += factor * values[one][tile]
        ratio_u, ratio_v = fixed[RATIO, here, :], fixed[RATIO + 1, here, :]
        for one in group:
            face_u[one].append(ratio_u * sums[one][0] + sums[one][2])
            face_v[one].append(ratio_v * sums[one][1] + sums[one][3])
            drags[one].append(sums[one][0] + sums[one][1])
    outs = []
    for one in group:
        totals = []
        for tile in range(count):
            total = face_u[one][tile] + west_of(face_u[one][tile]) + face_v[one][tile] + south_of(face_v[one], tile)
            if halo is not None and tile == halo - 1:
                total = total + fold_row(face_v[one][halo])
            totals.append(0.5 * total)
        outs.append((high[one], flow_u[one], flow_v[one], totals, drags[one]))
    return outs


STRIP_KEYS = tuple(
    (name, step) for name in ("traj_u", "traj_v", "wet_u", "wet_v") for step in range(3)
) + (("depth", None), ("drag", None), ("land", None))


def spread(packed):
    lane = iota(packed.shape, 1)
    arrays = [packed]
    for shift in (4 * GROUP, 2 * GROUP, GROUP):
        upper = (lane & shift) != 0
        halves = []
        for value in arrays:
            other = pltpu.roll(value, shift, 1)
            halves += [jnp.where(upper, other, value), jnp.where(upper, value, other)]
        arrays = halves
    return arrays


def shared_strips(values):
    strips = []
    for first in range(0, len(values), LANES // GROUP):
        some = values[first : first + LANES // GROUP]
        sides = [spread(packed) for packed in state_strips(some)]
        strips += [jnp.concatenate([sides[0][number], sides[1][number]], axis=1) for number in range(len(some))]
    return strips


def state_strips(values):
    lane = iota(values[0][0].shape, 1)
    sides = []
    for end in (-1, 0):
        strip = None
        for sens, pieces in enumerate(values):
            piece = pltpu.roll(pieces[end], GROUP * sens + GROUP // 2, 1)
            strip = piece if strip is None else jnp.where(lane >= GROUP * sens, piece, strip)
        sides.append(strip)
    return sides


def interior(*refs):
    held = dict(zip(NAMES, refs[:10]))
    results = refs[10:15]
    strips, strips_static, to_west, to_east = refs[15:19]
    moving, fixed = refs[19:21]
    sens_count, rows, width = held["adj_h"].shape
    count = rows // TILE

    def field(key, kind):
        name, step = key
        return (held[name][...] if held[name].ndim == 2 else held[name][step]).astype(jnp.float32)

    coefficients(field, None, moving, fixed)
    for number, strip in enumerate(shared_strips([lane_tiles(field(key, 0)) for key in STRIP_KEYS])):
        strips_static[number] = strip
    pack_columns(held, to_west, to_east)

    def each(turn, carry):
        first = turn * PAIR
        states = [
            tuple([held[name][first + one, rows_of(tile), :] for tile in range(count)] for name in NAMES[:3])
            for one in range(PAIR)
        ]
        for one, values in enumerate(march(states, moving, fixed, None, False)):
            for ref, tiles in zip(results, values):
                for tile in range(count):
                    ref[first + one, rows_of(tile), :] = tiles[tile]
        return carry

    lax.fori_loop(0, sens_count // PAIR, each, 0)
    for kind in range(3):
        values = [lane_tiles(held[NAMES[kind]][sens]) for sens in range(sens_count)]
        strips[kind] = jnp.concatenate(state_strips(values), axis=1)


def row_edges(*refs):
    held = dict(zip(NAMES, refs[:10]))
    halo, halo_static = refs[10:12]
    results = refs[17:22]
    outs = refs[22:27]
    strips, strips_static = refs[27:29]
    moving, fixed, sems = refs[29:32]
    _, at_top, _ = place()
    sens_count, rows, width = held["adj_h"].shape
    row = iota((TILE, width), 0)
    top, bottom = rows // TILE - 1, 0

    def shifted_halo(value, kind):
        if kind == 1:
            return jnp.where(at_top & (row < DEEP), pltpu.roll(value, width - 1, 1), value)
        return value

    def field(key, kind):
        name, step = key
        ref = held[name] if held[name].ndim == 2 else held[name].at[step]
        if key in TILES:
            between = shifted_halo(halo_static[TILES.index(key)], kind)
        else:
            between = jnp.ones((TILE, width), jnp.float32)
        parts = [ref[rows_of(top), :].astype(jnp.float32), between, ref[rows_of(bottom), :].astype(jnp.float32)]
        return jnp.concatenate(parts, axis=0)

    coefficients(field, 1, moving, fixed)

    def each(turn, carry):
        first = turn * PAIR
        states = []
        for one in range(PAIR):
            state = []
            for kind in range(3):
                ref = held[NAMES[kind]]
                between = shifted_halo(halo[3 * (first + one) + kind], kind)
                state.append([ref[first + one, rows_of(top), :], between, ref[first + one, rows_of(bottom), :]])
            states.append(tuple(state))
        for one, values in enumerate(march(states, moving, fixed, 1, at_top)):
            for ref, tiles in zip(results, values):
                ref[first + one, rows - DEEP :, :] = tiles[0][DEEP:]
                ref[first + one, :DEEP, :] = tiles[2][:DEEP]
        for one in range(PAIR):
            for number in range(5):
                middle = (first + one, slice(None), pl.ds(LANES, width - 2 * LANES))
                pltpu.make_async_copy(
                    results[number].at[middle], outs[number].at[middle], sems.at[number]
                ).start()
        return carry

    lax.fori_loop(0, sens_count // PAIR, each, 0)
    state = [
        state_strips([lane_tiles(halo[3 * sens + kind]) for sens in range(sens_count)]) for kind in range(3)
    ]
    static = shared_strips([lane_tiles(halo_static[index]) for index in range(len(TILES))])
    for kind in range(3):
        strips[kind] = jnp.concatenate(state[kind], axis=1)
    for index in range(len(TILES)):
        strips_static[index] = static[index]
    for number in range(5):
        middle = (slice(None), slice(None), pl.ds(LANES, width - 2 * LANES))
        pltpu.make_async_copy(results[number].at[middle], outs[number].at[middle], sems.at[number]).wait()


def column_edges(*refs):
    results = refs[:5]
    strips, strips_static, halo_strips, halo_strips_static, inner, outer = refs[5:11]
    outs = refs[16:21]
    ends, moving, fixed, sems = refs[21:25]
    _, at_top, _ = place()
    sens_count, rows, width = results[0].shape
    count = rows // TILE + 1
    last = count - 1
    half = GROUP // 2
    height = rows + TILE
    lane = iota((height, LANES), 1)
    within = lane & (GROUP - 1)
    row = iota((height, 2 * LANES), 0)

    west_inner = lax.axis_index("lon") % 2 == 1
    from_west = jnp.where(west_inner, inner[...], outer[...])
    from_east = jnp.where(west_inner, outer[...], inner[...])
    beyond = []
    for side in range(2):
        cols = slice(side * LANES, (side + 1) * LANES)
        easts = spread(pltpu.roll(from_east[:, cols], LANES + half - 3 * DEEP, 1))
        wests = spread(pltpu.roll(from_west[:, cols], LANES + DEEP - 3 * DEEP, 1))
        beyond += zip(easts, wests)

    def joined(own, halo_own, east, west, kind):
        own = jnp.concatenate([own, halo_own], axis=0)
        east = jnp.where(within < half, own[:, :LANES], east)
        west = jnp.where(within >= half, own[:, LANES:], west)
        value = jnp.concatenate([east, west], axis=1)
        if kind == 1:
            turned = pltpu.roll(value, 2 * LANES - 1, 1)
            value = jnp.where(at_top & (row >= rows) & (row < rows + DEEP), turned, value)
        return value

    def field(key, kind):
        name, step = key
        own = strips_static[STRIP_KEYS.index((name, None) if name == "drag" else key)]
        if key not in TILES:
            east = west = jnp.ones((height, LANES), jnp.float32)
            return joined(own, jnp.ones((TILE, 2 * LANES), jnp.float32), east, west, kind)
        index = TILES.index(key)
        east, west = beyond[index]
        return joined(own, halo_strips_static[index], east, west, kind)

    coefficients(field, last, moving, fixed)
    state = []
    for kind in range(3):
        east = pltpu.roll(from_east[:, :LANES], (half - DEEP * kind) % LANES, 1)
        west = pltpu.roll(from_west[:, :LANES], (DEEP - DEEP * kind) % LANES, 1)
        value = joined(strips[kind], halo_strips[kind], east, west, kind)
        state.append([value[rows_of(tile), :] for tile in range(count)])
    (values,) = march([tuple(state)], moving, fixed, last, at_top)
    copies = []
    lane = iota((rows, LANES), 1)
    for number in range(5):
        strip = jnp.concatenate(values[number][:last], axis=0)
        for side, first in ((0, width - LANES), (1, 0)):
            inside = lane >= LANES - DEEP if side == 0 else lane < DEEP
            part = strip[:, side * LANES : (side + 1) * LANES]
            merged = []
            for sens in range(sens_count):
                shift = (LANES - half - GROUP * sens) % LANES
                piece = pltpu.roll(part, shift, 1) if shift else part
                merged.append(jnp.where(inside, piece, results[number][sens, :, first : first + LANES]))
            for sens in range(sens_count):
                ends[side, number, sens] = merged[sens]
            copies.append(
                pltpu.make_async_copy(
                    ends.at[side, number], outs[number].at[:, :, pl.ds(first, LANES)], sems.at[side, number]
                )
            )
            copies[-1].start()
    for copy in copies:
        copy.wait()


def on_device(traj_u, traj_v, adj_h, adj_u, adj_v, depth, drag, land, wet_u, wet_v):
    count, rows, width = adj_h.shape
    steps = traj_u.shape[0]
    args = (adj_h, adj_u, adj_v, traj_u, traj_v, wet_u, wet_v, depth, drag, land)
    args = tuple(pltpu.with_memory_space_constraint(arg, pltpu.HBM) for arg in args)

    in_vmem = pl.BlockSpec(memory_space=pltpu.VMEM)
    in_hbm = pl.BlockSpec(memory_space=pl.ANY)
    params = pltpu.CompilerParams(vmem_limit_bytes=VMEM_LIMIT)
    row_pack = jax.ShapeDtypeStruct((message_rows(count), width), jnp.float32)
    *held, one, two = pl.pallas_call(
        pack_edges,
        in_specs=[in_hbm] * len(args),
        out_specs=[in_vmem] * (len(args) + 2),
        out_shape=[jax.ShapeDtypeStruct(arg.shape, arg.dtype) for arg in args] + [row_pack] * 2,
        scratch_shapes=[pltpu.SemaphoreType.DMA((len(args),))],
        compiler_params=params,
        name="pack_edges",
    )(*args)

    lons, lats, subs = (lax.axis_size(axis) for axis in GRID)
    total_rows = lats * subs

    def device(lon, row):
        return lon * total_rows + row

    route = [(device(lon, 0), device(lon ^ 1, 0)) for lon in range(lons)]
    for lon in range(lons):
        for row in range(1, total_rows - 1, 2):
            route += [(device(lon, row), device(lon, row + 1)), (device(lon, row + 1), device(lon, row))]
        route.append((device(lon, total_rows - 1), device(lons - 1 - lon, total_rows - 1)))
    two = lax.ppermute(two, GRID, route)

    one = lax.ppermute(one, "sub", [(core, core ^ 1) for core in range(subs)])

    def shape(*dims):
        return jax.ShapeDtypeStruct(dims, jnp.float32)

    def scratch(tiles, wide):
        return [
            pltpu.VMEM((8, steps, tiles * TILE, wide), jnp.float32),
            pltpu.VMEM((5, tiles * TILE, wide), jnp.float32),
        ]

    state = shape(*adj_h.shape)
    first = pl.pallas_call(
        interior,
        in_specs=[in_vmem] * 10,
        out_specs=[in_vmem] * 9,
        out_shape=[state] * 5
        + [shape(3, rows, 2 * LANES), shape(len(STRIP_KEYS), rows, 2 * LANES)]
        + [shape(rows, 2 * LANES)] * 2,
        scratch_shapes=scratch(rows // TILE, width),
        compiler_params=params,
        name="interior",
    )(*held)
    results, strips, own_columns = first[:5], first[5:7], first[7:]

    full_pack = jax.ShapeDtypeStruct((rows + TILE, 2 * LANES), jnp.float32)
    halo, halo_static, inner, outer = pl.pallas_call(
        merge_rows,
        out_shape=[
            shape(3 * count, TILE, width),
            shape(len(TILES), TILE, width),
            full_pack,
            full_pack,
        ],
        compiler_params=params,
        name="merge_rows",
    )(one, two, *own_columns)
    outer = lax.ppermute(outer, "lon", [(lon, (lon - 1 + 2 * (lon % 2)) % lons) for lon in range(lons)])
    inner = lax.ppermute(inner, "lon", [(lon, lon ^ 1) for lon in range(lons)])

    second = pl.pallas_call(
        row_edges,
        in_specs=[in_vmem] * 17,
        out_specs=[in_vmem] * 5 + [in_hbm] * 5 + [in_vmem] * 2,
        out_shape=[state] * 10 + [shape(3, TILE, 2 * LANES), shape(len(TILES), TILE, 2 * LANES)],
        input_output_aliases={12 + number: number for number in range(5)},
        scratch_shapes=scratch(3, width) + [pltpu.SemaphoreType.DMA((5,))],
        compiler_params=params,
        name="row_edges",
    )(*held, halo, halo_static, *results)
    results, outs, halo_strips = second[:5], second[5:10], second[10:]

    return pl.pallas_call(
        column_edges,
        in_specs=[in_vmem] * 11 + [in_hbm] * 5,
        out_specs=[in_hbm] * 5,
        out_shape=[state] * 5,
        input_output_aliases={11 + number: number for number in range(5)},
        scratch_shapes=[pltpu.VMEM((2, 5, count, rows, LANES), jnp.float32)]
        + scratch(rows // TILE + 1, 2 * LANES)
        + [pltpu.SemaphoreType.DMA((2, 5))],
        compiler_params=params,
        name="column_edges",
    )(*results, *strips, *halo_strips, inner, outer, *outs)


def solution(mesh):
    state = P("case", ROWS, "lon")
    fixed = P(ROWS, "lon")
    return jax.shard_map(
        on_device,
        mesh=mesh,
        in_specs=(state,) * 5 + (fixed,) * 3 + (state,) * 2,
        out_specs=(state,) * 5,
        check_vma=False,
    )
```

profile of v0, /device:TPU:0, one launch (start us, length us, event | category | flops | bytes accessed | tf_op | source)
XLA Modules:
  0.0 19.8 jit_solution(17151679012187350601)
XLA Ops:
  0.6 1.8 %pack_edges.1 = (f32[8,32,512]{2,1,0:T(8,128)S(1)}, f32[8,32,512]{2,1,0:T(8,128)S(1)}, f32[8,32,512]{2,1,0:T(8,128)S(1)}, f32[3,32,512]{2,1,0:T(8,128)S(1)}, f32...) custom-call(f32[8,32,512]{2,1,0:T(8,128)} %refs_0_.1, ...), custom_call_target="tpu_custom_call" | custom-call | tf_op jit(solution)/shard_map/pack_edges/pallas_call | solution.py:586
  2.5 0.5 %collective-permute-start = (f32[112,512]{1,0:T(8,128)S(1)}, f32[112,512]{1,0:T(8,128)S(1)}, u32[]{:S(2)}, u32[]{:S(2)}) collective-permute-start(f32[112,512]{1,0:T(8,128)S(1)} %get-tuple-element.52), channel_id=1, source_target_pairs={{0,1},{1,0},{2,3},{3,2},{4,5},{5,4},{6,7},{7,6},{8,9},{9,8},{10,11... | collective-permute-start | bytes 688136 | tf_op jit(solution)/shard_map/ppermute | solution.py:609
  3.0 2.6 %collective-permute-start.1 = (f32[112,512]{1,0:T(8,128)S(1)}, f32[112,512]{1,0:T(8,128)S(1)}, u32[]{:S(2)}, u32[]{:S(2)}) collective-permute-start(f32[112,512]{1,0:T(8,128)S(1)} %get-tuple-element.53), channel_id=1, source_target_pairs={{0,4},{4,0},{8,12},{12,8},{1,2},{2,1},{3,15},{5,6},{6,5},{7,11},{9... | collective-permute-start | bytes 688136 | tf_op jit(solution)/shard_map/ppermute | solution.py:607
  5.6 3.5 %interior.1 = (f32[8,32,512]{2,1,0:T(8,128)S(1)}, f32[8,32,512]{2,1,0:T(8,128)S(1)}, f32[8,32,512]{2,1,0:T(8,128)S(1)}, f32[8,32,512]{2,1,0:T(8,128)S(1)}, f32[8...) custom-call(f32[8,32,512]{2,1,0:T(8,128)S(1)} %get-tuple-element.42., ...), custom_call_target="tpu_custom_call" | custom-call | tf_op jit(solution)/shard_map/interior/pallas_call | solution.py:621
  9.1 0.0 collective-permute-done.one
  9.1 0.5 %collective-permute-done.1.two = f32[112,512]{1,0:T(8,128)S(1)} collective-permute-done((f32[112,512]{1,0:T(8,128)S(1)}, f32[112,512]{1,0:T(8,128)S(1)}, u32[]{:S(2)}, u32[]{:S(2)}) %collective-permute-start.1) | collective-permute-done | bytes 229408 | tf_op jit(solution)/shard_map/ppermute | solution.py:607
  9.6 0.2 %merge_rows.1 = (f32[24,8,512]{2,1,0:T(8,128)S(1)}, f32[14,8,512]{2,1,0:T(8,128)S(1)}, f32[40,256]{1,0:T(8,128)S(1)}, f32[40,256]{1,0:T(8,128)S(1)}) custom-call(f32[112,512]{1,0:T(8,128)S(1)} %collective-permute-done.one, f32[112,512]{1,0:T(8,128)S(1)} %collective-permute-done.1.two, f32[32,256]{1,0:T(8,128)S(1)} %get-tuple-element.54.own_west, ...), custom_call_target="tpu_custom_call" | custom-call | tf_op jit(solution)/shard_map/merge_rows/pallas_call | solution.py:635
  9.9 2.1 %collective-permute-start.2 = (f32[40,256]{1,0:T(8,128)S(1)}, f32[40,256]{1,0:T(8,128)S(1)}, u32[]{:S(2)}, u32[]{:S(2)}) collective-permute-start(f32[40,256]{1,0:T(8,128)S(1)} %get-tuple-element.72), channel_id=1, source_target_pairs={{0,4},{4,0},{8,12},{12,8},{1,5},{5,1},{9,13},{13,9},{2,6},{6,2},{1... | collective-permute-start | bytes 122888 | tf_op jit(solution)/shard_map/ppermute | solution.py:647
  12.0 2.5 %collective-permute-start.3 = (f32[40,256]{1,0:T(8,128)S(1)}, f32[40,256]{1,0:T(8,128)S(1)}, u32[]{:S(2)}, u32[]{:S(2)}) collective-permute-start(f32[40,256]{1,0:T(8,128)S(1)} %get-tuple-element.73), channel_id=1, source_target_pairs={{0,12},{4,8},{8,4},{12,0},{1,13},{5,9},{9,5},{13,1},{2,14},{6,10},... | collective-permute-start | bytes 122888 | tf_op jit(solution)/shard_map/ppermute | solution.py:646
  14.4 2.6 %row_edges.1 = (f32[8,32,512]{2,1,0:T(8,128)S(1)}, f32[8,32,512]{2,1,0:T(8,128)S(1)}, f32[8,32,512]{2,1,0:T(8,128)S(1)}, f32[8,32,512]{2,1,0:T(8,128)S(1)}, f32[...) custom-call(f32[8,32,512]{2,1,0:T(8,128)S(1)} %get-tuple-element.42., ...), custom_call_target="tpu_custom_call", output_to_operand_aliasing={{0}: (12, {}), {1}: (13, {}), {2}: (14, {}), {3}: (15, {}),... | custom-call | tf_op jit(solution)/shard_map/row_edges/pallas_call | solution.py:649
  17.0 0.0 collective-permute-done.2.refs_9_
  17.0 0.7 %collective-permute-done.3.refs_10_ = f32[40,256]{1,0:T(8,128)S(1)} collective-permute-done((f32[40,256]{1,0:T(8,128)S(1)}, f32[40,256]{1,0:T(8,128)S(1)}, u32[]{:S(2)}, u32[]{:S(2)}) %collective-permute-start.3) | collective-permute-done | bytes 40992 | tf_op jit(solution)/shard_map/ppermute | solution.py:646
  17.8 2.1 %column_edges.1 = (f32[8,32,512]{2,1,0:T(8,128)}, f32[8,32,512]{2,1,0:T(8,128)}, f32[8,32,512]{2,1,0:T(8,128)}, f32[8,32,512]{2,1,0:T(8,128)}, f32[8,32,512]{2,1,0:T(8,128)}) custom-call(f32[8,32,512]{2,1,0:T(8,128)S(1)} %get-tuple-element.63.refs_0_, ...), custom_call_target="tpu_custom_call", output_to_operand_aliasing={{0}: (11, {}), {1}: (12, {}), {2}: (13, {}), {3}: (14, {}),... | custom-call | tf_op jit(solution)/shard_map/column_edges/pallas_call | solution.py:661
Async XLA Ops:
  2.5 6.6 %collective-permute-start = (f32[112,512]{1,0:T(8,128)S(1)}, f32[112,512]{1,0:T(8,128)S(1)}, u32[]{:S(2)}, u32[]{:S(2)}) collective-permute-start(f32[112,512]{1,0:T(8,128)S(1)} %get-tuple-element.52), channel_id=1, source_target_pairs={{0,1},{1,0},{2,3},{3,2},{4,5},{5,4},{6,7},{7,6},{8,9},{9,8},{10,11... | collective-permute-start | bytes 688136 | tf_op jit(solution)/shard_map/ppermute | solution.py:609
  3.0 6.7 %collective-permute-start.1 = (f32[112,512]{1,0:T(8,128)S(1)}, f32[112,512]{1,0:T(8,128)S(1)}, u32[]{:S(2)}, u32[]{:S(2)}) collective-permute-start(f32[112,512]{1,0:T(8,128)S(1)} %get-tuple-element.53), channel_id=1, source_target_pairs={{0,4},{4,0},{8,12},{12,8},{1,2},{2,1},{3,15},{5,6},{6,5},{7,11},{9... | collective-permute-start | bytes 688136 | tf_op jit(solution)/shard_map/ppermute | solution.py:607
  9.9 7.2 %collective-permute-start.2 = (f32[40,256]{1,0:T(8,128)S(1)}, f32[40,256]{1,0:T(8,128)S(1)}, u32[]{:S(2)}, u32[]{:S(2)}) collective-permute-start(f32[40,256]{1,0:T(8,128)S(1)} %get-tuple-element.72), channel_id=1, source_target_pairs={{0,4},{4,0},{8,12},{12,8},{1,5},{5,1},{9,13},{13,9},{2,6},{6,2},{1... | collective-permute-start | bytes 122888 | tf_op jit(solution)/shard_map/ppermute | solution.py:647
  12.0 5.8 %collective-permute-start.3 = (f32[40,256]{1,0:T(8,128)S(1)}, f32[40,256]{1,0:T(8,128)S(1)}, u32[]{:S(2)}, u32[]{:S(2)}) collective-permute-start(f32[40,256]{1,0:T(8,128)S(1)} %get-tuple-element.73), channel_id=1, source_target_pairs={{0,12},{4,8},{8,4},{12,0},{1,13},{5,9},{9,5},{13,1},{2,14},{6,10},... | collective-permute-start | bytes 122888 | tf_op jit(solution)/shard_map/ppermute | solution.py:646
where the time goes:
time: 20 us; the launch traced here: 19.8 us
  Pallas kernels  10.2 us (51%)
  starting transfers between devices  7.73 us (39%)
  waiting for transfers between devices  1.23 us (6%)
  between operations  0.68 us (3%)
    pallas_call x1, Pallas kernels, on_device(): pl.pallas_call(interior, in_specs=[in_vmem] * 10, out_specs=[in_vmem] * 9...  3.46 us
    ppermute x1, starting transfers between devices, on_device(): two = lax.ppermute(two, GRID, route)  2.65 us
    pallas_call x1, Pallas kernels, on_device(): pl.pallas_call(row_edges, in_specs=[in_vmem] * 17, out_specs=[in_vmem] *...  2.6 us
    ppermute x1, starting transfers between devices, on_device(): lax.ppermute(outer, 'lon', [(lon, (lon - 1 + 2 * (lon % 2)) % lons) for l...  2.47 us
    ppermute x1, starting transfers between devices, on_device(): inner = lax.ppermute(inner, 'lon', [(lon, lon ^ 1) for lon in range(lons)])  2.09 us
    pallas_call x1, Pallas kernels, on_device(): pl.pallas_call(column_edges, in_specs=[in_vmem] * 11 + [in_hbm] * 5, out_...  2.08 us
    pallas_call x1, Pallas kernels, on_device(): pl.pallas_call(pack_edges, in_specs=[in_hbm] * len(args), out_specs=[in_v...  1.84 us
    ppermute x1, waiting for transfers between devices, on_device(): lax.ppermute(outer, 'lon', [(lon, (lon - 1 + 2 * (lon % 2)) % lons) for l...  0.7 us
  transfers between devices with their start and end apart: 4, of which 2 were waited for; matrix products, arithmetic and copies ran while one was open for 0% of the time, Pallas kernels for 31%

commit v1 on v0

--- a/solution.py
+++ b/solution.py
@@ -55,9 +55,12 @@
     return value.astype(jnp.float32)
 
 
+def message_size(count):
+    return sum(STATE_SLOTS) * count + sum(entry[2] for entry in SHARED)
+
+
 def message_rows(count):
-    rows = sum(STATE_SLOTS) * count + sum(entry[2] for entry in SHARED)
-    return -(-rows // TILE) * TILE
+    return -(-message_size(count) // TILE) * TILE
 
 
 def row_plan(count):
@@ -98,24 +101,32 @@
     return copies
 
 
-def edge(held, rows):
-    return {name: ref.at[(slice(None),) * (ref.ndim - 2) + (rows,)] for name, ref in held.items()}
-
-
-def pack_edges(*refs):
+def row_window(at_bottom_edge):
+    def window(rows, width):
+        first = pl.multiple_of(jnp.where(at_bottom_edge, 0, rows - TILE), TILE)
+        return pl.ds(first, TILE), slice(None)
+
+    return window
+
+
+def pack_edge(held, target, from_bottom, count):
+    for key, kind, turned, at, slots in row_plan(count):
+        value = masked(held, key)
+        target[at : at + slots, :] = jnp.where(from_bottom, value[:slots], value[TILE - slots :])
+
+
+def pack_far(*refs):
     arrays = dict(zip(NAMES, refs[:10]))
-    held = dict(zip(NAMES, refs[10:20]))
-    near, target, sems = refs[20:23]
+    target = refs[10]
+    held = dict(zip(NAMES, refs[11:21]))
     even, at_top, _ = place()
-    count, rows, width = arrays["adj_h"].shape
-    for copy in start_copies(arrays, held, sems, lambda rows, width: (slice(None), slice(None))).values():
+    count = arrays["adj_h"].shape[0]
+    for copy in start_copies(arrays, held, refs[21], row_window(even)).values():
         copy.wait()
-    low, held = edge(held, pl.ds(0, TILE)), edge(held, pl.ds(rows - TILE, TILE))
-    for key, kind, turned, at, slots in row_plan(count):
-        here = slice(at, at + slots)
-        south, north = masked(low, key)[:slots], masked(held, key)[TILE - slots :]
-        near[here, :] = jnp.where(even, north, south)
-        target[here, :] = jnp.where(even, south, north)
+
+    @pl.when(jnp.logical_not(at_top))
+    def _():
+        pack_edge(held, target, even, count)
 
     @pl.when(at_top)
     def _():
@@ -137,6 +148,19 @@
                     piece = jnp.where(row == slots - 1, piece, -piece) if kind == 2 else -piece
                 pieces.append(piece)
             target[at : at + slots, :] = jnp.concatenate(pieces, axis=1)[:slots]
+
+
+def pack_near(*refs):
+    args = dict(zip(NAMES, refs[:10]))
+    near = refs[11]
+    even, _, _ = place()
+    count, rows, width = args["adj_h"].shape
+    low, high = (
+        {name: ref.at[(slice(None),) * (ref.ndim - 2) + (pl.ds(first, TILE),)] for name, ref in args.items()}
+        for first in (0, rows - TILE)
+    )
+    for key, kind, turned, at, slots in row_plan(count):
+        near[at : at + slots, :] = jnp.where(even, masked(high, key)[TILE - slots :], masked(low, key)[:slots])
 
 
 def group_lanes(field, count):
@@ -577,21 +601,22 @@
     count, rows, width = adj_h.shape
     steps = traj_u.shape[0]
     args = (adj_h, adj_u, adj_v, traj_u, traj_v, wet_u, wet_v, depth, drag, land)
-    args = tuple(pltpu.with_memory_space_constraint(arg, pltpu.HBM) for arg in args)
+    in_hbm_args = tuple(pltpu.with_memory_space_constraint(arg, pltpu.HBM) for arg in args)
 
     in_vmem = pl.BlockSpec(memory_space=pltpu.VMEM)
     in_hbm = pl.BlockSpec(memory_space=pl.ANY)
     params = pltpu.CompilerParams(vmem_limit_bytes=VMEM_LIMIT)
     row_pack = jax.ShapeDtypeStruct((message_rows(count), width), jnp.float32)
-    *held, one, two = pl.pallas_call(
-        pack_edges,
+    packed = pl.pallas_call(
+        pack_far,
         in_specs=[in_hbm] * len(args),
-        out_specs=[in_vmem] * (len(args) + 2),
-        out_shape=[jax.ShapeDtypeStruct(arg.shape, arg.dtype) for arg in args] + [row_pack] * 2,
-        scratch_shapes=[pltpu.SemaphoreType.DMA((len(args),))],
+        out_specs=in_vmem,
+        out_shape=row_pack,
+        scratch_shapes=[pltpu.VMEM(arg.shape[:-2] + (TILE, width), arg.dtype) for arg in args]
+        + [pltpu.SemaphoreType.DMA((len(args),))],
         compiler_params=params,
-        name="pack_edges",
-    )(*args)
+        name="pack_far",
+    )(*in_hbm_args)
 
     lons, lats, subs = (lax.axis_size(axis) for axis in GRID)
     total_rows = lats * subs
@@ -604,9 +629,17 @@
         for row in range(1, total_rows - 1, 2):
             route += [(device(lon, row), device(lon, row + 1)), (device(lon, row + 1), device(lon, row))]
         route.append((device(lon, total_rows - 1), device(lons - 1 - lon, total_rows - 1)))
-    two = lax.ppermute(two, GRID, route)
-
+    two = lax.ppermute(packed, GRID, route)
+    one = pl.pallas_call(
+        pack_near,
+        in_specs=[in_vmem] * len(args) + [in_hbm],
+        out_specs=in_vmem,
+        out_shape=jax.ShapeDtypeStruct((message_size(count), width), jnp.float32),
+        compiler_params=params,
+        name="pack_near",
+    )(*args, packed)
     one = lax.ppermute(one, "sub", [(core, core ^ 1) for core in range(subs)])
+
 
     def shape(*dims):
         return jax.ShapeDtypeStruct(dims, jnp.float32)
@@ -628,7 +661,7 @@
         scratch_shapes=scratch(rows // TILE, width),
         compiler_params=params,
         name="interior",
-    )(*held)
+    )(*args)
     results, strips, own_columns = first[:5], first[5:7], first[7:]
 
     full_pack = jax.ShapeDtypeStruct((rows + TILE, 2 * LANES), jnp.float32)
@@ -655,7 +688,7 @@
         scratch_shapes=scratch(3, width) + [pltpu.SemaphoreType.DMA((5,))],
         compiler_params=params,
         name="row_edges",
-    )(*held, halo, halo_static, *results)
+    )(*args, halo, halo_static, *results)
     results, outs, halo_strips = second[:5], second[5:10], second[10:]
 
     return pl.pallas_call(

time: 20 us -> 19.6 us (0.980)
  Pallas kernels: 10.2 us -> 9.86 us
  waiting for transfers between devices: 1.23 us -> 0.94 us
    ppermute x1, starting transfers between devices: 2.65 us -> 3.09 us  [on_device(): two = lax.ppermute(packed, GRID, route)]
    ppermute x1, starting transfers between devices: 0.52 us -> 0.1 us  [on_device(): one = lax.ppermute(one, 'sub', [(core, core ^ 1) for core in range(subs)])]
    pallas_call x1 -> x2, Pallas kernels: 1.84 us -> 1.52 us  [the longest x1 1.4 us: on_device(): pl.pallas_call(pack_far, in_specs=[in_hbm] * len(args), out_specs=in_vmem...]
    ppermute x1, waiting for transfers between devices: 0.52 us -> 0.23 us  [on_device(): two = lax.ppermute(packed, GRID, route)]
  transfers between devices with their start and end apart: 4 -> 4, of which waited for: 2 -> 2; matrix products, arithmetic and copies ran while one was open for 0% -> 0% of each run, Pallas kernels for 31% -> 32%
where the time goes in v1:
time: 19.6 us; the launch traced here: 19.4 us
  Pallas kernels  9.86 us (50%)
  starting transfers between devices  7.74 us (39%)
  waiting for transfers between devices  0.94 us (5%)
  between operations  0.81 us (4%)
    pallas_call x1, Pallas kernels, on_device(): pl.pallas_call(interior, in_specs=[in_vmem] * 10, out_specs=[in_vmem] * 9...  3.46 us
    ppermute x1, starting transfers between devices, on_device(): two = lax.ppermute(packed, GRID, route)  3.09 us
    pallas_call x1, Pallas kernels, on_device(): pl.pallas_call(row_edges, in_specs=[in_vmem] * 17, out_specs=[in_vmem] *...  2.6 us
    ppermute x1, starting transfers between devices, on_device(): lax.ppermute(outer, 'lon', [(lon, (lon - 1 + 2 * (lon % 2)) % lons) for l...  2.47 us
    ppermute x1, starting transfers between devices, on_device(): inner = lax.ppermute(inner, 'lon', [(lon, lon ^ 1) for lon in range(lons)])  2.09 us
    pallas_call x1, Pallas kernels, on_device(): pl.pallas_call(column_edges, in_specs=[in_vmem] * 11 + [in_hbm] * 5, out_...  2.07 us
    pallas_call x1, Pallas kernels, on_device(): pl.pallas_call(pack_far, in_specs=[in_hbm] * len(args), out_specs=in_vmem...  1.4 us
    ppermute x1, waiting for transfers between devices, on_device(): lax.ppermute(outer, 'lon', [(lon, (lon - 1 + 2 * (lon % 2)) % lons) for l...  0.7 us
  transfers between devices with their start and end apart: 4, of which 2 were waited for; matrix products, arithmetic and copies ran while one was open for 0% of the time, Pallas kernels for 32%

profile of v1, /device:TPU:0, one launch (start us, length us, event | category | flops | bytes accessed | tf_op | source)
XLA Modules:
  0.0 19.4 jit_solution(16217394007509742522)
XLA Ops:
  0.6 0.0 copy-start.6
  0.6 0.0 copy-start.5
  0.7 0.0 copy-start.9
  0.7 0.0 copy-start.8
  0.7 0.0 copy-start.7
  0.7 0.0 copy-start.2
  0.7 0.0 copy-start.1
  0.7 0.0 copy-start
  0.7 0.0 copy-start.4
  0.7 0.0 copy-start.3
  0.7 1.4 %pack_far.1.refs_10_ = f32[112,512]{1,0:T(8,128)S(1)} custom-call(f32[8,32,512]{2,1,0:T(8,128)} %refs_0_.7, f32[8,32,512]{2,1,0:T(8,128)} %refs_1_.7, f32[8,32,512]{2,1,0:T(8,128)} %refs_2_.7, f32[3,32,512]{2,1,0:T(8,128)} %refs_3_.7, f32[3,32,512]{2,1,0:T(8,128)} %refs_4_.7, s32[3,32,512]{2,1,0:T(8,128)} %refs_5_.7, s32[3,32,512]{2,1,0:T(8,128)} %refs_6_.7, ...), custom_call_target="tpu_custom_call" | custom-call | tf_op jit(solution)/shard_map/pack_far/pallas_call | solution.py:610
  2.1 3.1 %collective-permute-start.1 = (f32[112,512]{1,0:T(8,128)S(1)}, f32[112,512]{1,0:T(8,128)S(1)}, u32[]{:S(2)}, u32[]{:S(2)}) collective-permute-start(f32[112,512]{1,0:T(8,128)S(1)} %pack_far.1.refs_10_), channel_id=1, source_target_pairs={{0,4},{4,0},{8,12},{12,8},{1,2},{2,1},{3,15},{5,6},{6,5},{7,11},{9... | collective-permute-start | bytes 688136 | tf_op jit(solution)/shard_map/ppermute | solution.py:632
  5.3 0.1 pack_near.1
  5.4 0.1 collective-permute-start
  5.5 3.5 %interior.1 = (f32[8,32,512]{2,1,0:T(8,128)S(1)}, f32[8,32,512]{2,1,0:T(8,128)S(1)}, f32[8,32,512]{2,1,0:T(8,128)S(1)}, f32[8,32,512]{2,1,0:T(8,128)S(1)}, f32[8...) custom-call(f32[8,32,512]{2,1,0:T(8,128)S(1)} %copy-done, ...), custom_call_target="tpu_custom_call" | custom-call | tf_op jit(solution)/shard_map/interior/pallas_call | solution.py:654
  9.0 0.0 collective-permute-done.one
  9.0 0.2 %collective-permute-done.1.two = f32[112,512]{1,0:T(8,128)S(1)} collective-permute-done((f32[112,512]{1,0:T(8,128)S(1)}, f32[112,512]{1,0:T(8,128)S(1)}, u32[]{:S(2)}, u32[]{:S(2)}) %collective-permute-start.1) | collective-permute-done | bytes 229408 | tf_op jit(solution)/shard_map/ppermute | solution.py:632
  9.2 0.2 %merge_rows.1 = (f32[24,8,512]{2,1,0:T(8,128)S(1)}, f32[14,8,512]{2,1,0:T(8,128)S(1)}, f32[40,256]{1,0:T(8,128)S(1)}, f32[40,256]{1,0:T(8,128)S(1)}) custom-call(f32[106,512]{1,0:T(8,128)S(1)} %collective-permute-done.one, f32[112,512]{1,0:T(8,128)S(1)} %collective-permute-done.1.two, f32[32,256]{1,0:T(8,128)S(1)} %get-tuple-element.30.own_west, ...), custom_call_target="tpu_custom_call" | custom-call | tf_op jit(solution)/shard_map/merge_rows/pallas_call | solution.py:668
  9.4 2.1 %collective-permute-start.2 = (f32[40,256]{1,0:T(8,128)S(1)}, f32[40,256]{1,0:T(8,128)S(1)}, u32[]{:S(2)}, u32[]{:S(2)}) collective-permute-start(f32[40,256]{1,0:T(8,128)S(1)} %get-tuple-element.48), channel_id=1, source_target_pairs={{0,4},{4,0},{8,12},{12,8},{1,5},{5,1},{9,13},{13,9},{2,6},{6,2},{1... | collective-permute-start | bytes 122888 | tf_op jit(solution)/shard_map/ppermute | solution.py:680
  11.5 2.5 %collective-permute-start.3 = (f32[40,256]{1,0:T(8,128)S(1)}, f32[40,256]{1,0:T(8,128)S(1)}, u32[]{:S(2)}, u32[]{:S(2)}) collective-permute-start(f32[40,256]{1,0:T(8,128)S(1)} %get-tuple-element.49), channel_id=1, source_target_pairs={{0,12},{4,8},{8,4},{12,0},{1,13},{5,9},{9,5},{13,1},{2,14},{6,10},... | collective-permute-start | bytes 122888 | tf_op jit(solution)/shard_map/ppermute | solution.py:679
  14.0 2.6 %row_edges.1 = (f32[8,32,512]{2,1,0:T(8,128)S(1)}, f32[8,32,512]{2,1,0:T(8,128)S(1)}, f32[8,32,512]{2,1,0:T(8,128)S(1)}, f32[8,32,512]{2,1,0:T(8,128)S(1)}, f32[...) custom-call(f32[8,32,512]{2,1,0:T(8,128)S(1)} %copy-done, ...), custom_call_target="tpu_custom_call", output_to_operand_aliasing={{0}: (12, {}), {1}: (13, {}), {2}: (14, {}), {3}: (15, {}),... | custom-call | tf_op jit(solution)/shard_map/row_edges/pallas_call | solution.py:682
  16.6 0.0 collective-permute-done.2.refs_9_
  16.6 0.7 %collective-permute-done.3.refs_10_ = f32[40,256]{1,0:T(8,128)S(1)} collective-permute-done((f32[40,256]{1,0:T(8,128)S(1)}, f32[40,256]{1,0:T(8,128)S(1)}, u32[]{:S(2)}, u32[]{:S(2)}) %collective-permute-start.3) | collective-permute-done | bytes 40992 | tf_op jit(solution)/shard_map/ppermute | solution.py:679
  17.3 2.1 %column_edges.1 = (f32[8,32,512]{2,1,0:T(8,128)}, f32[8,32,512]{2,1,0:T(8,128)}, f32[8,32,512]{2,1,0:T(8,128)}, f32[8,32,512]{2,1,0:T(8,128)}, f32[8,32,512]{2,1,0:T(8,128)}) custom-call(f32[8,32,512]{2,1,0:T(8,128)S(1)} %get-tuple-element.39.refs_0_, ...), custom_call_target="tpu_custom_call", output_to_operand_aliasing={{0}: (11, {}), {1}: (12, {}), {2}: (13, {}), {3}: (14, {}),... | custom-call | tf_op jit(solution)/shard_map/column_edges/pallas_call | solution.py:694
  (10 shorter events, 0.0 us)
Async XLA Ops:
  0.6 4.6 %copy-start.6 = (s32[3,32,512]{2,1,0:T(8,128)S(1)}, s32[3,32,512]{2,1,0:T(8,128)}, u32[]{:S(2)}) copy-start(s32[3,32,512]{2,1,0:T(8,128)} %refs_6_.7) | copy-start | bytes 589828
  0.6 4.6 %copy-start.5 = (s32[3,32,512]{2,1,0:T(8,128)S(1)}, s32[3,32,512]{2,1,0:T(8,128)}, u32[]{:S(2)}) copy-start(s32[3,32,512]{2,1,0:T(8,128)} %refs_5_.7) | copy-start | bytes 589828
  0.7 4.6 %copy-start.9 = (s32[32,512]{1,0:T(8,128)S(1)}, s32[32,512]{1,0:T(8,128)}, u32[]{:S(2)}) copy-start(s32[32,512]{1,0:T(8,128)} %refs_9_.7) | copy-start | bytes 196612
  0.7 4.6 %copy-start.8 = (f32[32,512]{1,0:T(8,128)S(1)}, f32[32,512]{1,0:T(8,128)}, u32[]{:S(2)}) copy-start(f32[32,512]{1,0:T(8,128)} %refs_8_.7) | copy-start | bytes 196612
  0.7 4.6 %copy-start.7 = (f32[32,512]{1,0:T(8,128)S(1)}, f32[32,512]{1,0:T(8,128)}, u32[]{:S(2)}) copy-start(f32[32,512]{1,0:T(8,128)} %refs_7_.7) | copy-start | bytes 196612
  0.7 4.6 %copy-start.2 = (f32[8,32,512]{2,1,0:T(8,128)S(1)}, f32[8,32,512]{2,1,0:T(8,128)}, u32[]{:S(2)}) copy-start(f32[8,32,512]{2,1,0:T(8,128)} %refs_2_.7) | copy-start | bytes 1572868
  0.7 4.6 %copy-start.1 = (f32[8,32,512]{2,1,0:T(8,128)S(1)}, f32[8,32,512]{2,1,0:T(8,128)}, u32[]{:S(2)}) copy-start(f32[8,32,512]{2,1,0:T(8,128)} %refs_1_.7) | copy-start | bytes 1572868
  0.7 4.6 %copy-start = (f32[8,32,512]{2,1,0:T(8,128)S(1)}, f32[8,32,512]{2,1,0:T(8,128)}, u32[]{:S(2)}) copy-start(f32[8,32,512]{2,1,0:T(8,128)} %refs_0_.7) | copy-start | bytes 1572868
  0.7 4.6 %copy-start.4 = (f32[3,32,512]{2,1,0:T(8,128)S(1)}, f32[3,32,512]{2,1,0:T(8,128)}, u32[]{:S(2)}) copy-start(f32[3,32,512]{2,1,0:T(8,128)} %refs_4_.7) | copy-start | bytes 589828
  0.7 4.6 %copy-start.3 = (f32[3,32,512]{2,1,0:T(8,128)S(1)}, f32[3,32,512]{2,1,0:T(8,128)}, u32[]{:S(2)}) copy-start(f32[3,32,512]{2,1,0:T(8,128)} %refs_3_.7) | copy-start | bytes 589828
  2.1 7.1 %collective-permute-start.1 = (f32[112,512]{1,0:T(8,128)S(1)}, f32[112,512]{1,0:T(8,128)S(1)}, u32[]{:S(2)}, u32[]{:S(2)}) collective-permute-start(f32[112,512]{1,0:T(8,128)S(1)} %pack_far.1.refs_10_), channel_id=1, source_target_pairs={{0,4},{4,0},{8,12},{12,8},{1,2},{2,1},{3,15},{5,6},{6,5},{7,11},{9... | collective-permute-start | bytes 688136 | tf_op jit(solution)/shard_map/ppermute | solution.py:632
  5.4 3.6 %collective-permute-start = (f32[106,512]{1,0:T(8,128)S(1)}, f32[106,512]{1,0:T(8,128)S(1)}, u32[]{:S(2)}, u32[]{:S(2)}) collective-permute-start(f32[106,512]{1,0:T(8,128)S(1)} %pack_near.1), channel_id=1, source_target_pairs={{0,1},{1,0},{2,3},{3,2},{4,5},{5,4},{6,7},{7,6},{8,9},{9,8},{10,11... | collective-permute-start | bytes 651272 | tf_op jit(solution)/shard_map/ppermute | solution.py:641
  9.4 7.2 %collective-permute-start.2 = (f32[40,256]{1,0:T(8,128)S(1)}, f32[40,256]{1,0:T(8,128)S(1)}, u32[]{:S(2)}, u32[]{:S(2)}) collective-permute-start(f32[40,256]{1,0:T(8,128)S(1)} %get-tuple-element.48), channel_id=1, source_target_pairs={{0,4},{4,0},{8,12},{12,8},{1,5},{5,1},{9,13},{13,9},{2,6},{6,2},{1... | collective-permute-start | bytes 122888 | tf_op jit(solution)/shard_map/ppermute | solution.py:680
  11.5 5.8 %collective-permute-start.3 = (f32[40,256]{1,0:T(8,128)S(1)}, f32[40,256]{1,0:T(8,128)S(1)}, u32[]{:S(2)}, u32[]{:S(2)}) collective-permute-start(f32[40,256]{1,0:T(8,128)S(1)} %get-tuple-element.49), channel_id=1, source_target_pairs={{0,12},{4,8},{8,4},{12,0},{1,13},{5,9},{9,5},{13,1},{2,14},{6,10},... | collective-permute-start | bytes 122888 | tf_op jit(solution)/shard_map/ppermute | solution.py:679

commit v2 on v1

--- a/solution.py
+++ b/solution.py
@@ -17,7 +17,7 @@
 LANES = 128
 DEEP = 4
 GROUP = 16
-PAIR = 4
+PAIR = 8
 VMEM_LIMIT = 48 * 1024 * 1024
 
 
@@ -192,15 +192,14 @@
             target[:, side * LANES : (side + 1) * LANES] = packed[side]
 
 
-def merge_rows(one, two, own_west, own_east, halo, halo_static, inner, outer):
+def merge_rows(one, two, own_west, own_east, halo, halo_static, to_west, to_east):
     even, at_top, at_bottom = place()
     width = one.shape[1]
     rows = own_west.shape[0]
     count = halo.shape[0] // 3
     lane = iota((TILE, LANES), 1)
-    west_inner = lax.axis_index("lon") % 2 == 1
-    inner[:rows, :] = jnp.where(west_inner, own_west[...], own_east[...])
-    outer[:rows, :] = jnp.where(west_inner, own_east[...], own_west[...])
+    to_west[:rows, :] = own_west[...]
+    to_east[:rows, :] = own_east[...]
     field = 0
     tiles = []
     for key, kind, turned, at, slots in row_plan(count):
@@ -237,9 +236,8 @@
             packed[way][side] = piece if held is None else jnp.where(lane >= start, piece, held)
     for side in range(2):
         cols = slice(side * LANES, (side + 1) * LANES)
-        west, east = packed[0][side], packed[1][side]
-        inner[rows:, cols] = jnp.where(west_inner, west, east)
-        outer[rows:, cols] = jnp.where(west_inner, east, west)
+        to_west[rows:, cols] = packed[0][side]
+        to_east[rows:, cols] = packed[1][side]
 
 
 def rows_of(tile):
@@ -466,6 +464,13 @@
     sens_count, rows, width = held["adj_h"].shape
     row = iota((TILE, width), 0)
     top, bottom = rows // TILE - 1, 0
+    inside = (slice(None), pl.ds(TILE, rows - 2 * TILE), pl.ds(LANES, width - 2 * LANES))
+    copies = [
+        pltpu.make_async_copy(results[number].at[inside], outs[number].at[inside], sems.at[number])
+        for number in range(5)
+    ]
+    for copy in copies:
+        copy.start()
 
     def shifted_halo(value, kind):
         if kind == 1:
@@ -498,12 +503,6 @@
             for ref, tiles in zip(results, values):
                 ref[first + one, rows - DEEP :, :] = tiles[0][DEEP:]
                 ref[first + one, :DEEP, :] = tiles[2][:DEEP]
-        for one in range(PAIR):
-            for number in range(5):
-                middle = (first + one, slice(None), pl.ds(LANES, width - 2 * LANES))
-                pltpu.make_async_copy(
-                    results[number].at[middle], outs[number].at[middle], sems.at[number]
-                ).start()
         return carry
 
     lax.fori_loop(0, sens_count // PAIR, each, 0)
@@ -515,14 +514,13 @@
         strips[kind] = jnp.concatenate(state[kind], axis=1)
     for index in range(len(TILES)):
         strips_static[index] = static[index]
-    for number in range(5):
-        middle = (slice(None), slice(None), pl.ds(LANES, width - 2 * LANES))
-        pltpu.make_async_copy(results[number].at[middle], outs[number].at[middle], sems.at[number]).wait()
+    for copy in copies:
+        copy.wait()
 
 
 def column_edges(*refs):
     results = refs[:5]
-    strips, strips_static, halo_strips, halo_strips_static, inner, outer = refs[5:11]
+    strips, strips_static, halo_strips, halo_strips_static, from_west_ref, from_east_ref = refs[5:11]
     outs = refs[16:21]
     ends, moving, fixed, sems = refs[21:25]
     _, at_top, _ = place()
@@ -535,9 +533,15 @@
     within = lane & (GROUP - 1)
     row = iota((height, 2 * LANES), 0)
 
-    west_inner = lax.axis_index("lon") % 2 == 1
-    from_west = jnp.where(west_inner, inner[...], outer[...])
-    from_east = jnp.where(west_inner, outer[...], inner[...])
+    copies = []
+    for number in range(5):
+        for side, first in enumerate((0, rows - TILE)):
+            middle = (slice(None), pl.ds(first, TILE), pl.ds(LANES, width - 2 * LANES))
+            copies.append(
+                pltpu.make_async_copy(results[number].at[middle], outs[number].at[middle], sems.at[2 + side, number])
+            )
+            copies[-1].start()
+    from_west, from_east = from_west_ref[...], from_east_ref[...]
     beyond = []
     for side in range(2):
         cols = slice(side * LANES, (side + 1) * LANES)
@@ -573,7 +577,6 @@
         value = joined(strips[kind], halo_strips[kind], east, west, kind)
         state.append([value[rows_of(tile), :] for tile in range(count)])
     (values,) = march([tuple(state)], moving, fixed, last, at_top)
-    copies = []
     lane = iota((rows, LANES), 1)
     for number in range(5):
         strip = jnp.concatenate(values[number][:last], axis=0)
@@ -665,7 +668,7 @@
     results, strips, own_columns = first[:5], first[5:7], first[7:]
 
     full_pack = jax.ShapeDtypeStruct((rows + TILE, 2 * LANES), jnp.float32)
-    halo, halo_static, inner, outer = pl.pallas_call(
+    halo, halo_static, to_west, to_east = pl.pallas_call(
         merge_rows,
         out_shape=[
             shape(3 * count, TILE, width),
@@ -676,8 +679,8 @@
         compiler_params=params,
         name="merge_rows",
     )(one, two, *own_columns)
-    outer = lax.ppermute(outer, "lon", [(lon, (lon - 1 + 2 * (lon % 2)) % lons) for lon in range(lons)])
-    inner = lax.ppermute(inner, "lon", [(lon, lon ^ 1) for lon in range(lons)])
+    from_west = lax.ppermute(to_east, "lon", [(lon, (lon + 1) % lons) for lon in range(lons)])
+    from_east = lax.ppermute(to_west, "lon", [(lon, (lon - 1) % lons) for lon in range(lons)])
 
     second = pl.pallas_call(
         row_edges,
@@ -699,10 +702,10 @@
         input_output_aliases={11 + number: number for number in range(5)},
         scratch_shapes=[pltpu.VMEM((2, 5, count, rows, LANES), jnp.float32)]
         + scratch(rows // TILE + 1, 2 * LANES)
-        + [pltpu.SemaphoreType.DMA((2, 5))],
+        + [pltpu.SemaphoreType.DMA((4, 5))],
         compiler_params=params,
         name="column_edges",
-    )(*results, *strips, *halo_strips, inner, outer, *outs)
+    )(*results, *strips, *halo_strips, from_west, from_east, *outs)
 
 
 def solution(mesh):

time: 19.6 us -> 18.3 us (0.934)
  Pallas kernels: 9.86 us -> 9.02 us
  starting transfers between devices: 7.74 us -> 7.35 us
    pallas_call x1, Pallas kernels: 2.6 us -> 1.8 us  [on_device(): pl.pallas_call(row_edges, in_specs=[in_vmem] * 17, out_specs=[in_vmem] *...]
    ppermute x2, starting transfers between devices: 4.56 us -> 4.16 us  [the longest x1 2.09 us: on_device(): lax.ppermute(to_west, 'lon', [(lon, (lon - 1) % lons) for lon in range(lo...]
  transfers between devices with their start and end apart: 4 -> 4, of which waited for: 2 -> 3; matrix products, arithmetic and copies ran while one was open for 0% -> 0% of each run, Pallas kernels for 32% -> 29%
where the time goes in v2:
time: 18.3 us; the launch traced here: 18.1 us
  Pallas kernels  9.02 us (49%)
  starting transfers between devices  7.35 us (40%)
  waiting for transfers between devices  0.91 us (5%)
  between operations  0.81 us (4%)
    pallas_call x1, Pallas kernels, on_device(): pl.pallas_call(interior, in_specs=[in_vmem] * 10, out_specs=[in_vmem] * 9...  3.33 us
    ppermute x1, starting transfers between devices, on_device(): two = lax.ppermute(packed, GRID, route)  3.09 us
    pallas_call x1, Pallas kernels, on_device(): pl.pallas_call(column_edges, in_specs=[in_vmem] * 11 + [in_hbm] * 5, out_...  2.16 us
    ppermute x1, starting transfers between devices, on_device(): lax.ppermute(to_west, 'lon', [(lon, (lon - 1) % lons) for lon in range(lo...  2.09 us
    ppermute x1, starting transfers between devices, on_device(): lax.ppermute(to_east, 'lon', [(lon, (lon + 1) % lons) for lon in range(lo...  2.07 us
    pallas_call x1, Pallas kernels, on_device(): pl.pallas_call(row_edges, in_specs=[in_vmem] * 17, out_specs=[in_vmem] *...  1.8 us
    pallas_call x1, Pallas kernels, on_device(): pl.pallas_call(pack_far, in_specs=[in_hbm] * len(args), out_specs=in_vmem...  1.4 us
  transfers between devices with their start and end apart: 4, of which 3 were waited for; matrix products, arithmetic and copies ran while one was open for 0% of the time, Pallas kernels for 29%

profile of v2, /device:TPU:0, one launch (start us, length us, event | category | flops | bytes accessed | tf_op | source)
XLA Modules:
  0.0 18.1 jit_solution(16742815141442188600)
XLA Ops:
  0.6 0.0 copy-start.6
  0.6 0.0 copy-start.5
  0.7 0.0 copy-start.9
  0.7 0.0 copy-start.8
  0.7 0.0 copy-start.7
  0.7 0.0 copy-start.2
  0.7 0.0 copy-start.1
  0.7 0.0 copy-start
  0.7 0.0 copy-start.4
  0.7 1.4 %pack_far.1.refs_10_ = f32[112,512]{1,0:T(8,128)S(1)} custom-call(f32[8,32,512]{2,1,0:T(8,128)} %refs_0_.7, f32[8,32,512]{2,1,0:T(8,128)} %refs_1_.7, f32[8,32,512]{2,1,0:T(8,128)} %refs_2_.7, f32[3,32,512]{2,1,0:T(8,128)} %refs_3_.7, f32[3,32,512]{2,1,0:T(8,128)} %refs_4_.7, s32[3,32,512]{2,1,0:T(8,128)} %refs_5_.7, s32[3,32,512]{2,1,0:T(8,128)} %refs_6_.7, ...), custom_call_target="tpu_custom_call" | custom-call | tf_op jit(solution)/shard_map/pack_far/pallas_call | solution.py:613
  2.1 3.1 %collective-permute-start.1 = (f32[112,512]{1,0:T(8,128)S(1)}, f32[112,512]{1,0:T(8,128)S(1)}, u32[]{:S(2)}, u32[]{:S(2)}) collective-permute-start(f32[112,512]{1,0:T(8,128)S(1)} %pack_far.1.refs_10_), channel_id=1, source_target_pairs={{0,4},{4,0},{8,12},{12,8},{1,2},{2,1},{3,15},{5,6},{6,5},{7,11},{9... | collective-permute-start | bytes 688136 | tf_op jit(solution)/shard_map/ppermute | solution.py:635
  5.2 0.0 copy-done.9
  5.3 0.1 pack_near.1
  5.4 0.1 collective-permute-start
  5.5 3.3 %interior.1 = (f32[8,32,512]{2,1,0:T(8,128)S(1)}, f32[8,32,512]{2,1,0:T(8,128)S(1)}, f32[8,32,512]{2,1,0:T(8,128)S(1)}, f32[8,32,512]{2,1,0:T(8,128)S(1)}, f32[8...) custom-call(f32[8,32,512]{2,1,0:T(8,128)S(1)} %copy-done, ...), custom_call_target="tpu_custom_call" | custom-call | tf_op jit(solution)/shard_map/interior/pallas_call | solution.py:657
  8.9 0.0 collective-permute-done.one
  8.9 0.4 %collective-permute-done.1.two = f32[112,512]{1,0:T(8,128)S(1)} collective-permute-done((f32[112,512]{1,0:T(8,128)S(1)}, f32[112,512]{1,0:T(8,128)S(1)}, u32[]{:S(2)}, u32[]{:S(2)}) %collective-permute-start.1) | collective-permute-done | bytes 229408 | tf_op jit(solution)/shard_map/ppermute | solution.py:635
  9.2 0.2 %merge_rows.1 = (f32[24,8,512]{2,1,0:T(8,128)S(1)}, f32[14,8,512]{2,1,0:T(8,128)S(1)}, f32[40,256]{1,0:T(8,128)S(1)}, f32[40,256]{1,0:T(8,128)S(1)}) custom-call(f32[106,512]{1,0:T(8,128)S(1)} %collective-permute-done.one, f32[112,512]{1,0:T(8,128)S(1)} %collective-permute-done.1.two, f32[32,256]{1,0:T(8,128)S(1)} %get-tuple-element.30.own_west, ...), custom_call_target="tpu_custom_call" | custom-call | tf_op jit(solution)/shard_map/merge_rows/pallas_call | solution.py:671
  9.5 2.1 %collective-permute-start.2 = (f32[40,256]{1,0:T(8,128)S(1)}, f32[40,256]{1,0:T(8,128)S(1)}, u32[]{:S(2)}, u32[]{:S(2)}) collective-permute-start(f32[40,256]{1,0:T(8,128)S(1)} %get-tuple-element.48), channel_id=1, source_target_pairs={{0,4},{4,8},{8,12},{12,0},{1,5},{5,9},{9,13},{13,1},{2,6},{6,10},{... | collective-permute-start | bytes 122888 | tf_op jit(solution)/shard_map/ppermute | solution.py:682
  11.5 2.1 %collective-permute-start.3 = (f32[40,256]{1,0:T(8,128)S(1)}, f32[40,256]{1,0:T(8,128)S(1)}, u32[]{:S(2)}, u32[]{:S(2)}) collective-permute-start(f32[40,256]{1,0:T(8,128)S(1)} %get-tuple-element.49), channel_id=1, source_target_pairs={{0,12},{4,0},{8,4},{12,8},{1,13},{5,1},{9,5},{13,9},{2,14},{6,2},{... | collective-permute-start | bytes 122888 | tf_op jit(solution)/shard_map/ppermute | solution.py:683
  13.6 1.8 %row_edges.1 = (f32[8,32,512]{2,1,0:T(8,128)S(1)}, f32[8,32,512]{2,1,0:T(8,128)S(1)}, f32[8,32,512]{2,1,0:T(8,128)S(1)}, f32[8,32,512]{2,1,0:T(8,128)S(1)}, f32[...) custom-call(f32[8,32,512]{2,1,0:T(8,128)S(1)} %copy-done, ...), custom_call_target="tpu_custom_call", output_to_operand_aliasing={{0}: (12, {}), {1}: (13, {}), {2}: (14, {}), {3}: (15, {}),... | custom-call | tf_op jit(solution)/shard_map/row_edges/pallas_call | solution.py:685
  15.4 0.3 %collective-permute-done.2.refs_9_ = f32[40,256]{1,0:T(8,128)S(1)} collective-permute-done((f32[40,256]{1,0:T(8,128)S(1)}, f32[40,256]{1,0:T(8,128)S(1)}, u32[]{:S(2)}, u32[]{:S(2)}) %collective-permute-start.2) | collective-permute-done | bytes 40992 | tf_op jit(solution)/shard_map/ppermute | solution.py:682
  15.7 0.3 %collective-permute-done.3.refs_10_ = f32[40,256]{1,0:T(8,128)S(1)} collective-permute-done((f32[40,256]{1,0:T(8,128)S(1)}, f32[40,256]{1,0:T(8,128)S(1)}, u32[]{:S(2)}, u32[]{:S(2)}) %collective-permute-start.3) | collective-permute-done | bytes 40992 | tf_op jit(solution)/shard_map/ppermute | solution.py:683
  16.0 2.2 %column_edges.1 = (f32[8,32,512]{2,1,0:T(8,128)}, f32[8,32,512]{2,1,0:T(8,128)}, f32[8,32,512]{2,1,0:T(8,128)}, f32[8,32,512]{2,1,0:T(8,128)}, f32[8,32,512]{2,1,0:T(8,128)}) custom-call(f32[8,32,512]{2,1,0:T(8,128)S(1)} %get-tuple-element.39.refs_0_, ...), custom_call_target="tpu_custom_call", output_to_operand_aliasing={{0}: (11, {}), {1}: (12, {}), {2}: (13, {}), {3}: (14, {}),... | custom-call | tf_op jit(solution)/shard_map/column_edges/pallas_call | solution.py:697
  (10 shorter events, 0.0 us)
Async XLA Ops:
  0.6 4.6 %copy-start.6 = (s32[3,32,512]{2,1,0:T(8,128)S(1)}, s32[3,32,512]{2,1,0:T(8,128)}, u32[]{:S(2)}) copy-start(s32[3,32,512]{2,1,0:T(8,128)} %refs_6_.7) | copy-start | bytes 589828
  0.6 4.6 %copy-start.5 = (s32[3,32,512]{2,1,0:T(8,128)S(1)}, s32[3,32,512]{2,1,0:T(8,128)}, u32[]{:S(2)}) copy-start(s32[3,32,512]{2,1,0:T(8,128)} %refs_5_.7) | copy-start | bytes 589828
  0.7 4.6 %copy-start.9 = (s32[32,512]{1,0:T(8,128)S(1)}, s32[32,512]{1,0:T(8,128)}, u32[]{:S(2)}) copy-start(s32[32,512]{1,0:T(8,128)} %refs_9_.7) | copy-start | bytes 196612
  0.7 4.6 %copy-start.8 = (f32[32,512]{1,0:T(8,128)S(1)}, f32[32,512]{1,0:T(8,128)}, u32[]{:S(2)}) copy-start(f32[32,512]{1,0:T(8,128)} %refs_8_.7) | copy-start | bytes 196612
  0.7 4.6 %copy-start.7 = (f32[32,512]{1,0:T(8,128)S(1)}, f32[32,512]{1,0:T(8,128)}, u32[]{:S(2)}) copy-start(f32[32,512]{1,0:T(8,128)} %refs_7_.7) | copy-start | bytes 196612
  0.7 4.6 %copy-start.2 = (f32[8,32,512]{2,1,0:T(8,128)S(1)}, f32[8,32,512]{2,1,0:T(8,128)}, u32[]{:S(2)}) copy-start(f32[8,32,512]{2,1,0:T(8,128)} %refs_2_.7) | copy-start | bytes 1572868
  0.7 4.6 %copy-start.1 = (f32[8,32,512]{2,1,0:T(8,128)S(1)}, f32[8,32,512]{2,1,0:T(8,128)}, u32[]{:S(2)}) copy-start(f32[8,32,512]{2,1,0:T(8,128)} %refs_1_.7) | copy-start | bytes 1572868
  0.7 4.6 %copy-start = (f32[8,32,512]{2,1,0:T(8,128)S(1)}, f32[8,32,512]{2,1,0:T(8,128)}, u32[]{:S(2)}) copy-start(f32[8,32,512]{2,1,0:T(8,128)} %refs_0_.7) | copy-start | bytes 1572868
  0.7 4.6 %copy-start.4 = (f32[3,32,512]{2,1,0:T(8,128)S(1)}, f32[3,32,512]{2,1,0:T(8,128)}, u32[]{:S(2)}) copy-start(f32[3,32,512]{2,1,0:T(8,128)} %refs_4_.7) | copy-start | bytes 589828
  0.7 4.6 %copy-start.3 = (f32[3,32,512]{2,1,0:T(8,128)S(1)}, f32[3,32,512]{2,1,0:T(8,128)}, u32[]{:S(2)}) copy-start(f32[3,32,512]{2,1,0:T(8,128)} %refs_3_.7) | copy-start | bytes 589828
  2.1 7.1 %collective-permute-start.1 = (f32[112,512]{1,0:T(8,128)S(1)}, f32[112,512]{1,0:T(8,128)S(1)}, u32[]{:S(2)}, u32[]{:S(2)}) collective-permute-start(f32[112,512]{1,0:T(8,128)S(1)} %pack_far.1.refs_10_), channel_id=1, source_target_pairs={{0,4},{4,0},{8,12},{12,8},{1,2},{2,1},{3,15},{5,6},{6,5},{7,11},{9... | collective-permute-start | bytes 688136 | tf_op jit(solution)/shard_map/ppermute | solution.py:635
  5.4 3.4 %collective-permute-start = (f32[106,512]{1,0:T(8,128)S(1)}, f32[106,512]{1,0:T(8,128)S(1)}, u32[]{:S(2)}, u32[]{:S(2)}) collective-permute-start(f32[106,512]{1,0:T(8,128)S(1)} %pack_near.1), channel_id=1, source_target_pairs={{0,1},{1,0},{2,3},{3,2},{4,5},{5,4},{6,7},{7,6},{8,9},{9,8},{10,11... | collective-permute-start | bytes 651272 | tf_op jit(solution)/shard_map/ppermute | solution.py:644
  9.5 6.3 %collective-permute-start.2 = (f32[40,256]{1,0:T(8,128)S(1)}, f32[40,256]{1,0:T(8,128)S(1)}, u32[]{:S(2)}, u32[]{:S(2)}) collective-permute-start(f32[40,256]{1,0:T(8,128)S(1)} %get-tuple-element.48), channel_id=1, source_target_pairs={{0,4},{4,8},{8,12},{12,0},{1,5},{5,9},{9,13},{13,1},{2,6},{6,10},{... | collective-permute-start | bytes 122888 | tf_op jit(solution)/shard_map/ppermute | solution.py:682
  11.5 4.4 %collective-permute-start.3 = (f32[40,256]{1,0:T(8,128)S(1)}, f32[40,256]{1,0:T(8,128)S(1)}, u32[]{:S(2)}, u32[]{:S(2)}) collective-permute-start(f32[40,256]{1,0:T(8,128)S(1)} %get-tuple-element.49), channel_id=1, source_target_pairs={{0,12},{4,0},{8,4},{12,8},{1,13},{5,1},{9,5},{13,9},{2,14},{6,2},{... | collective-permute-start | bytes 122888 | tf_op jit(solution)/shard_map/ppermute | solution.py:683

commit v3 on v2

--- a/solution.py
+++ b/solution.py
@@ -31,7 +31,7 @@
     return row % 2 == 0, row == last, row == 0
 
 
-STATE_SLOTS = (3, 3, 4)
+STATE_ROWS = 8
 SHARED = (
     (("traj_v", 2), 2, 3, True),
     (("traj_v", 1), 2, 2, True),
@@ -55,24 +55,20 @@
     return value.astype(jnp.float32)
 
 
-def message_size(count):
-    return sum(STATE_SLOTS) * count + sum(entry[2] for entry in SHARED)
-
-
-def message_rows(count):
-    return -(-message_size(count) // TILE) * TILE
-
-
-def row_plan(count):
-    plan, at = [], 0
-    for sens in range(count):
-        for kind in range(3):
-            plan.append(((NAMES[kind], sens), kind, kind > 0, at, STATE_SLOTS[kind]))
-            at += STATE_SLOTS[kind]
+def message_size(count, width):
+    return STATE_ROWS * count + sum(entry[2] for entry in SHARED) + -(-count // (width // LANES))
+
+
+def message_rows(count, width):
+    return -(-message_size(count, width) // TILE) * TILE
+
+
+def shared_plan(count):
+    plan, at = [], STATE_ROWS * count
     for key, kind, slots, turned in SHARED:
         plan.append((key, kind, turned, at, slots))
         at += slots
-    return plan
+    return plan, at
 
 
 def lane_tiles(value):
@@ -109,10 +105,65 @@
     return window
 
 
-def pack_edge(held, target, from_bottom, count):
-    for key, kind, turned, at, slots in row_plan(count):
-        value = masked(held, key)
-        target[at : at + slots, :] = jnp.where(from_bottom, value[:slots], value[TILE - slots :])
+LOW, HIGH, FOLD = range(3)
+
+
+def edge_rows(value, slots, mode, kind=0, turned=False):
+    if mode == LOW:
+        return [value[:slots]]
+    if mode == HIGH:
+        return [value[TILE - slots :]]
+    if kind == 2:
+        order = [TILE - 2 - slot for slot in range(slots - 1)] + [TILE - 1]
+    else:
+        order = [TILE - 1 - slot for slot in range(slots)]
+    picked = [value[source : source + 1] for source in order]
+    if turned:
+        picked = [-row for row in picked[: slots - 1]] + picked[slots - 1 :] if kind == 2 else [-row for row in picked]
+    return picked
+
+
+def pack_edge(held, target, mode):
+    count, _, width = held["adj_h"].shape
+    lane = iota((TILE, width), 1)
+    across = LANES - 1 - iota((TILE, LANES), 1)
+    third = 2 if mode == LOW else TILE - 3
+
+    def mirrored(value):
+        if mode != FOLD:
+            return value
+        rows = []
+        for first in range(0, value.shape[0], TILE):
+            pieces = lane_tiles(value[first : first + TILE])[::-1]
+            rows.append(jnp.concatenate([jnp.take_along_axis(piece, across, axis=1) for piece in pieces], axis=1))
+        return jnp.concatenate(rows, axis=0)
+
+    ends = []
+    for sens in range(count):
+        high, flow_u, flow_v = (masked(held, (name, sens)) for name in NAMES[:3])
+        west = jnp.where(lane == 0, 0.0, pltpu.roll(flow_u, 1, 1))
+        ahead = high + 0.5 * (flow_u - west + flow_v - pltpu.roll(flow_v, 1, 0))
+        rows = edge_rows(high, 2, mode)
+        rows += edge_rows(flow_u, 2, mode, 1, True)
+        rows += edge_rows(flow_v, 3, mode, 2, True)
+        rows.append(ahead[third : third + 1])
+        here = slice(STATE_ROWS * sens, STATE_ROWS * (sens + 1))
+        target[here, :] = mirrored(jnp.concatenate(rows, axis=0))
+        end = flow_u[third : third + 1, width - LANES :]
+        ends.append(-end if mode == FOLD else end)
+    rows = []
+    plan, _ = shared_plan(count)
+    for key, kind, turned, at, slots in plan:
+        rows += edge_rows(masked(held, key), slots, mode, kind, turned)
+    each = width // LANES
+    for first in range(0, count, each):
+        some = ends[first : first + each]
+        blank = [jnp.zeros((1, LANES), jnp.float32)] * (each - len(some))
+        rows.append(jnp.concatenate(some + blank, axis=1))
+    rows.append(jnp.zeros((message_rows(count, width) - message_size(count, width), width), jnp.float32))
+    shared = mirrored(jnp.concatenate([row for row in rows if row.shape[0]], axis=0))
+    size = target.shape[0] - STATE_ROWS * count
+    target[STATE_ROWS * count :, :] = shared[:size]
 
 
 def pack_far(*refs):
@@ -120,34 +171,20 @@
     target = refs[10]
     held = dict(zip(NAMES, refs[11:21]))
     even, at_top, _ = place()
-    count = arrays["adj_h"].shape[0]
     for copy in start_copies(arrays, held, refs[21], row_window(even)).values():
         copy.wait()
 
-    @pl.when(jnp.logical_not(at_top))
+    @pl.when(even)
     def _():
-        pack_edge(held, target, even, count)
+        pack_edge(held, target, LOW)
+
+    @pl.when(jnp.logical_not(even) & jnp.logical_not(at_top))
+    def _():
+        pack_edge(held, target, HIGH)
 
     @pl.when(at_top)
     def _():
-        row = iota((TILE, LANES), 0)
-        lane = LANES - 1 - iota((TILE, LANES), 1)
-        for key, kind, turned, at, slots in row_plan(count):
-            value = masked(held, key)
-            sources = [TILE - 1 - slot for slot in range(slots)]
-            if kind == 2:
-                sources = [TILE - 2 - slot for slot in range(slots - 1)] + [TILE - 1]
-            order = jnp.zeros((TILE, LANES), jnp.int32)
-            for slot, source in enumerate(sources):
-                order = jnp.where(row == slot, source, order)
-            pieces = []
-            for piece in lane_tiles(value)[::-1]:
-                piece = jnp.take_along_axis(piece, lane, axis=1)
-                piece = jnp.take_along_axis(piece, order, axis=0)
-                if turned:
-                    piece = jnp.where(row == slots - 1, piece, -piece) if kind == 2 else -piece
-                pieces.append(piece)
-            target[at : at + slots, :] = jnp.concatenate(pieces, axis=1)[:slots]
+        pack_edge(held, target, FOLD)
 
 
 def pack_near(*refs):
@@ -159,37 +196,56 @@
         {name: ref.at[(slice(None),) * (ref.ndim - 2) + (pl.ds(first, TILE),)] for name, ref in args.items()}
         for first in (0, rows - TILE)
     )
-    for key, kind, turned, at, slots in row_plan(count):
-        near[at : at + slots, :] = jnp.where(even, masked(high, key)[TILE - slots :], masked(low, key)[:slots])
-
-
-def group_lanes(field, count):
-    if field < 3 * count:
-        return 0, GROUP * (field // 3) + DEEP * (field % 3)
-    static = field - 3 * count
-    return static // count, GROUP * (static % count) + 3 * DEEP
+
+    @pl.when(even)
+    def _():
+        pack_edge(high, near, HIGH)
+
+    @pl.when(jnp.logical_not(even))
+    def _():
+        pack_edge(low, near, LOW)
+
+
+COLUMN_SLOTS = {
+    ("traj_u", 2): (0, 0, 3),
+    ("traj_u", 0): (0, 3, 1),
+    ("wet_u", 1): (1, 0, 3),
+    ("depth", None): (2, 0, 3),
+    ("drag", 1): (3, 0, 3),
+    ("land", None): (4, 0, 3),
+    ("traj_u", 1): (5, 0, 2),
+    ("wet_u", 0): (5, 2, 2),
+    ("traj_v", 2): (6, 0, 2),
+    ("wet_v", 1): (6, 2, 2),
+    ("drag", 2): (7, 0, 2),
+    ("traj_v", 1): (7, 2, 1),
+    ("wet_v", 0): (7, 3, 1),
+}
 
 
 def column_fields(count):
-    keys = [(NAMES[kind], sens) for sens in range(count) for kind in range(3)] + list(TILES)
-    fields = [(key,) + group_lanes(field, count) + (field,) for field, key in enumerate(keys)]
-    return sorted(fields, key=lambda entry: entry[1:])
+    fields = []
+    for sens in range(count):
+        for kind in range(3):
+            fields.append(((NAMES[kind], sens), GROUP * sens + DEEP * kind, DEEP, 3 * sens + kind))
+    for key, (slot, offset, columns) in COLUMN_SLOTS.items():
+        fields.append((key, GROUP * slot + 3 * DEEP + offset, columns, 3 * count + TILES.index(key)))
+    return sorted(fields, key=lambda entry: entry[1])
 
 
 def pack_columns(held, to_west, to_east):
     count, rows, width = held["adj_h"].shape
     lane = iota((rows, LANES), 1)
-    for target, first, origin in ((to_west, 0, 0), (to_east, width - LANES, LANES - DEEP)):
+    for target, first, east in ((to_west, 0, False), (to_east, width - LANES, True)):
         side_held = {name: ref.at[(slice(None),) * (ref.ndim - 1) + (pl.ds(first, LANES),)] for name, ref in held.items()}
-        packed = [None, None]
-        for key, side, at, _ in column_fields(count):
+        packed = None
+        for key, start, columns, _ in column_fields(count):
             value = masked(side_held, key)
-            shift = (at - origin) % LANES
+            shift = (start + columns) % LANES if east else start
             if shift:
                 value = pltpu.roll(value, shift, 1)
-            packed[side] = value if packed[side] is None else jnp.where(lane >= at, value, packed[side])
-        for side in range(2):
-            target[:, side * LANES : (side + 1) * LANES] = packed[side]
+            packed = value if packed is None else jnp.where(lane >= start, value, packed)
+        target[...] = packed
 
 
 def merge_rows(one, two, own_west, own_east, halo, halo_static, to_west, to_east):
@@ -200,44 +256,63 @@
     lane = iota((TILE, LANES), 1)
     to_west[:rows, :] = own_west[...]
     to_east[:rows, :] = own_east[...]
-    field = 0
-    tiles = []
-    for key, kind, turned, at, slots in row_plan(count):
-        here = slice(at, at + slots)
+
+    def beyond(here):
         north = jnp.where(even, one[here, :], two[here, :])
         south = jnp.where(even, two[here, :], one[here, :])
-        south = jnp.where(at_bottom, 0.0, south)
-        blank = jnp.zeros((DEEP - slots, width), jnp.float32)
-        gap = [blank] if slots < DEEP else []
+        return north, jnp.where(at_bottom, 0.0, south)
+
+    def blank(slots, columns=width):
+        return jnp.zeros((slots, columns), jnp.float32)
+
+    plan, ends_at = shared_plan(count)
+    each = width // LANES
+    tiles, ends = [], []
+    for sens in range(count):
+        north, south = beyond(slice(STATE_ROWS * sens, STATE_ROWS * (sens + 1)))
+        third_north = north[7:8] + 0.5 * north[5:6]
+        third_south = south[7:8] - 0.5 * south[4:5]
+        fold = jnp.where(at_top, north[6:7], 0.0)
+        tiles.append(jnp.concatenate([north[:2], third_north, blank(2), third_south, south[:2]], axis=0))
+        tiles.append(jnp.concatenate([north[2:4], blank(4), south[2:4]], axis=0))
+        tiles.append(jnp.concatenate([north[4:6], blank(1), fold, blank(1), south[4:7]], axis=0))
+        end_north, end_south = beyond(slice(ends_at + sens // each, ends_at + sens // each + 1))
+        mine, turned = (slice(number * LANES, (number + 1) * LANES) for number in (sens % each, each - 1 - sens % each))
+        end_north = jnp.where(at_top, end_north[:, turned], end_north[:, mine])
+        west = [blank(2, LANES), jnp.where(at_top, end_north, 0.0), blank(5, LANES)]
+        east = [blank(2, LANES), jnp.where(at_top, 0.0, end_north), blank(2, LANES), end_south[:, mine], blank(2, LANES)]
+        ends.append((jnp.concatenate(west, axis=0), jnp.concatenate(east, axis=0)))
+    for key, kind, turned, at, slots in plan:
+        north, south = beyond(slice(at, at + slots))
+        gap = [blank(DEEP - slots)] if slots < DEEP else []
         plain = jnp.concatenate([north] + gap + gap + [south], axis=0)
         values = [plain]
         if kind >= 2 and slots < DEEP:
             fold = ([north[:-1]] if slots > 1 else []) + gap + [north[-1:]] + gap + [south]
             if kind == 3:
-                fold = [north[1:], blank, north[:1]] + gap + [south]
+                fold = [north[1:], blank(1), north[:1]] + gap + [south]
                 values.append(jnp.where(at_top, jnp.concatenate(fold, axis=0), plain))
             else:
                 values = [jnp.where(at_top, jnp.concatenate(fold, axis=0), plain)]
         tiles += values
-    tiles.append(jnp.zeros((TILE, width), jnp.float32))
+    tiles.append(blank(TILE))
     for field, value in enumerate(tiles):
         if field < halo.shape[0]:
             halo[field] = value
         else:
             halo_static[field - halo.shape[0]] = value
-    packed = [[None, None], [None, None]]
-    for key, side, start, field in column_fields(count):
+    packed = [None, None]
+    for key, start, columns, field in column_fields(count):
         pieces = lane_tiles(tiles[field])
-        for way, piece, origin in ((0, pieces[0], 0), (1, pieces[-1], LANES - DEEP)):
-            shift = (start - origin) % LANES
+        if field < 3 * count and field % 3 == 1:
+            west, east = ends[field // 3]
+            pieces = [pieces[0] + west, pieces[-1] + east]
+        for way, piece, shift in ((0, pieces[0], start), (1, pieces[-1], (start + columns) % LANES)):
             if shift:
                 piece = pltpu.roll(piece, shift, 1)
-            held = packed[way][side]
-            packed[way][side] = piece if held is None else jnp.where(lane >= start, piece, held)
-    for side in range(2):
-        cols = slice(side * LANES, (side + 1) * LANES)
-        to_west[rows:, cols] = packed[0][side]
-        to_east[rows:, cols] = packed[1][side]
+            packed[way] = piece if packed[way] is None else jnp.where(lane >= start, piece, packed[way])
+    to_west[rows:, :] = packed[0]
+    to_east[rows:, :] = packed[1]
 
 
 def rows_of(tile):
@@ -269,8 +344,9 @@
         for step in range(3):
             now = field(("traj_" + way, step), kind)
             square = now * now
-            speed = jnp.sqrt(square + speed_floor)
-            keep = 2.0 + ratio * (speed + square / speed)
+            root = lax.rsqrt(square + speed_floor)
+            speed = (square + speed_floor) * root
+            keep = 2.0 + ratio * (speed + square * root)
             deep = face
             if step > 0:
                 mask = 0.5 * wet[step - 1]
@@ -542,12 +618,8 @@
             )
             copies[-1].start()
     from_west, from_east = from_west_ref[...], from_east_ref[...]
-    beyond = []
-    for side in range(2):
-        cols = slice(side * LANES, (side + 1) * LANES)
-        easts = spread(pltpu.roll(from_east[:, cols], LANES + half - 3 * DEEP, 1))
-        wests = spread(pltpu.roll(from_west[:, cols], LANES + DEEP - 3 * DEEP, 1))
-        beyond += zip(easts, wests)
+    easts = spread(pltpu.roll(from_east, LANES + half - 3 * DEEP, 1))
+    wests = spread(pltpu.roll(from_west, LANES + DEEP - 3 * DEEP, 1))
 
     def joined(own, halo_own, east, west, kind):
         own = jnp.concatenate([own, halo_own], axis=0)
@@ -565,9 +637,15 @@
         if key not in TILES:
             east = west = jnp.ones((height, LANES), jnp.float32)
             return joined(own, jnp.ones((TILE, 2 * LANES), jnp.float32), east, west, kind)
-        index = TILES.index(key)
-        east, west = beyond[index]
-        return joined(own, halo_strips_static[index], east, west, kind)
+        east = west = jnp.zeros((height, LANES), jnp.float32)
+        if key in COLUMN_SLOTS:
+            slot, offset, columns = COLUMN_SLOTS[key]
+            east, west = easts[slot], wests[slot]
+            if offset:
+                east = pltpu.roll(east, LANES - offset, 1)
+            if columns + offset < DEEP:
+                west = pltpu.roll(west, DEEP - columns - offset, 1)
+        return joined(own, halo_strips_static[TILES.index(key)], east, west, kind)
 
     coefficients(field, last, moving, fixed)
     state = []
@@ -609,7 +687,7 @@
     in_vmem = pl.BlockSpec(memory_space=pltpu.VMEM)
     in_hbm = pl.BlockSpec(memory_space=pl.ANY)
     params = pltpu.CompilerParams(vmem_limit_bytes=VMEM_LIMIT)
-    row_pack = jax.ShapeDtypeStruct((message_rows(count), width), jnp.float32)
+    row_pack = jax.ShapeDtypeStruct((message_rows(count, width), width), jnp.float32)
     packed = pl.pallas_call(
         pack_far,
         in_specs=[in_hbm] * len(args),
@@ -637,7 +715,7 @@
         pack_near,
         in_specs=[in_vmem] * len(args) + [in_hbm],
         out_specs=in_vmem,
-        out_shape=jax.ShapeDtypeStruct((message_size(count), width), jnp.float32),
+        out_shape=jax.ShapeDtypeStruct((message_size(count, width), width), jnp.float32),
         compiler_params=params,
         name="pack_near",
     )(*args, packed)
@@ -660,14 +738,14 @@
         out_specs=[in_vmem] * 9,
         out_shape=[state] * 5
         + [shape(3, rows, 2 * LANES), shape(len(STRIP_KEYS), rows, 2 * LANES)]
-        + [shape(rows, 2 * LANES)] * 2,
+        + [shape(rows, LANES)] * 2,
         scratch_shapes=scratch(rows // TILE, width),
         compiler_params=params,
         name="interior",
     )(*args)
     results, strips, own_columns = first[:5], first[5:7], first[7:]
 
-    full_pack = jax.ShapeDtypeStruct((rows + TILE, 2 * LANES), jnp.float32)
+    full_pack = jax.ShapeDtypeStruct((rows + TILE, LANES), jnp.float32)
     halo, halo_static, to_west, to_east = pl.pallas_call(
         merge_rows,
         out_shape=[

time: 18.3 us -> 17.6 us (0.962)
  waiting for transfers between devices: 0.91 us -> 0.12 us
    ppermute x1, waiting for transfers between devices: 0.36 us -> 0.01 us  [on_device(): two = lax.ppermute(packed, GRID, route)]
    ppermute x1, waiting for transfers between devices: 0.28 us -> 0.03 us  [on_device(): lax.ppermute(to_east, 'lon', [(lon, (lon + 1) % lons) for lon in range(lo...]
  transfers between devices with their start and end apart: 4 -> 4, of which waited for: 3 -> 1; matrix products, arithmetic and copies ran while one was open for 0% -> 0% of each run, Pallas kernels for 29% -> 30%
where the time goes in v3:
time: 17.6 us; the launch traced here: 17.4 us
  Pallas kernels  9.16 us (52%)
  starting transfers between devices  7.26 us (41%)
  between operations  0.82 us (5%)
    pallas_call x1, Pallas kernels, on_device(): pl.pallas_call(interior, in_specs=[in_vmem] * 10, out_specs=[in_vmem] * 9...  3.36 us
    ppermute x1, starting transfers between devices, on_device(): two = lax.ppermute(packed, GRID, route)  3.09 us
    pallas_call x1, Pallas kernels, on_device(): pl.pallas_call(column_edges, in_specs=[in_vmem] * 11 + [in_hbm] * 5, out_...  2.15 us
    ppermute x1, starting transfers between devices, on_device(): lax.ppermute(to_west, 'lon', [(lon, (lon - 1) % lons) for lon in range(lo...  2.09 us
    ppermute x1, starting transfers between devices, on_device(): lax.ppermute(to_east, 'lon', [(lon, (lon + 1) % lons) for lon in range(lo...  1.99 us
    pallas_call x1, Pallas kernels, on_device(): pl.pallas_call(row_edges, in_specs=[in_vmem] * 17, out_specs=[in_vmem] *...  1.78 us
    pallas_call x1, Pallas kernels, on_device(): pl.pallas_call(pack_far, in_specs=[in_hbm] * len(args), out_specs=in_vmem...  1.46 us
  transfers between devices with their start and end apart: 4, of which 1 were waited for; matrix products, arithmetic and copies ran while one was open for 0% of the time, Pallas kernels for 30%

profile of v3, /device:TPU:0, one launch (start us, length us, event | category | flops | bytes accessed | tf_op | source)
XLA Modules:
  0.0 17.4 jit_solution(16482577683727410985)
XLA Ops:
  0.6 0.0 copy-start.6
  0.6 0.0 copy-start.5
  0.7 0.0 copy-start.9
  0.7 0.0 copy-start.8
  0.7 0.0 copy-start.7
  0.7 0.0 copy-start.2
  0.7 0.0 copy-start.1
  0.7 0.0 copy-start
  0.7 0.0 copy-start.4
  0.7 1.5 %pack_far.1.refs_10_ = f32[96,512]{1,0:T(8,128)S(1)} custom-call(f32[8,32,512]{2,1,0:T(8,128)} %refs_0_.7, f32[8,32,512]{2,1,0:T(8,128)} %refs_1_.7, f32[8,32,512]{2,1,0:T(8,128)} %refs_2_.7, f32[3,32,512]{2,1,0:T(8,128)} %refs_3_.7, f32[3,32,512]{2,1,0:T(8,128)} %refs_4_.7, s32[3,32,512]{2,1,0:T(8,128)} %refs_5_.7, s32[3,32,512]{2,1,0:T(8,128)} %refs_6_.7, ...), custom_call_target="tpu_custom_call" | custom-call | tf_op jit(solution)/shard_map/pack_far/pallas_call | solution.py:691
  2.2 3.1 %collective-permute-start.1 = (f32[96,512]{1,0:T(8,128)S(1)}, f32[96,512]{1,0:T(8,128)S(1)}, u32[]{:S(2)}, u32[]{:S(2)}) collective-permute-start(f32[96,512]{1,0:T(8,128)S(1)} %pack_far.1.refs_10_), channel_id=1, source_target_pairs={{0,4},{4,0},{8,12},{12,8},{1,2},{2,1},{3,15},{5,6},{6,5},{7,11},{9... | collective-permute-start | bytes 589832 | tf_op jit(solution)/shard_map/ppermute | solution.py:713
  5.3 0.0 copy-done.5
  5.4 0.2 pack_near.1
  5.5 0.1 collective-permute-start
  5.6 3.4 %interior.1 = (f32[8,32,512]{2,1,0:T(8,128)S(1)}, f32[8,32,512]{2,1,0:T(8,128)S(1)}, f32[8,32,512]{2,1,0:T(8,128)S(1)}, f32[8,32,512]{2,1,0:T(8,128)S(1)}, f32[8...) custom-call(f32[8,32,512]{2,1,0:T(8,128)S(1)} %copy-done, ...), custom_call_target="tpu_custom_call" | custom-call | tf_op jit(solution)/shard_map/interior/pallas_call | solution.py:735
  9.0 0.0 collective-permute-done.one
  9.0 0.0 collective-permute-done.1.two
  9.0 0.3 %merge_rows.1 = (f32[24,8,512]{2,1,0:T(8,128)S(1)}, f32[14,8,512]{2,1,0:T(8,128)S(1)}, f32[40,128]{1,0:T(8,128)S(1)}, f32[40,128]{1,0:T(8,128)S(1)}) custom-call(f32[92,512]{1,0:T(8,128)S(1)} %collective-permute-done.one, f32[96,512]{1,0:T(8,128)S(1)} %collective-permute-done.1.two, f32[32,128]{1,0:T(8,128)S(1)} %get-tuple-element.30.own_west, ...), custom_call_target="tpu_custom_call" | custom-call | tf_op jit(solution)/shard_map/merge_rows/pallas_call | solution.py:749
  9.3 2.0 %collective-permute-start.2 = (f32[40,128]{1,0:T(8,128)S(1)}, f32[40,128]{1,0:T(8,128)S(1)}, u32[]{:S(2)}, u32[]{:S(2)}) collective-permute-start(f32[40,128]{1,0:T(8,128)S(1)} %get-tuple-element.48), channel_id=1, source_target_pairs={{0,4},{4,8},{8,12},{12,0},{1,5},{5,9},{9,13},{13,1},{2,6},{6,10},{... | collective-permute-start | bytes 61448 | tf_op jit(solution)/shard_map/ppermute | solution.py:760
  11.3 2.1 %collective-permute-start.3 = (f32[40,128]{1,0:T(8,128)S(1)}, f32[40,128]{1,0:T(8,128)S(1)}, u32[]{:S(2)}, u32[]{:S(2)}) collective-permute-start(f32[40,128]{1,0:T(8,128)S(1)} %get-tuple-element.49), channel_id=1, source_target_pairs={{0,12},{4,0},{8,4},{12,8},{1,13},{5,1},{9,5},{13,9},{2,14},{6,2},{... | collective-permute-start | bytes 61448 | tf_op jit(solution)/shard_map/ppermute | solution.py:761
  13.4 1.8 %row_edges.1 = (f32[8,32,512]{2,1,0:T(8,128)S(1)}, f32[8,32,512]{2,1,0:T(8,128)S(1)}, f32[8,32,512]{2,1,0:T(8,128)S(1)}, f32[8,32,512]{2,1,0:T(8,128)S(1)}, f32[...) custom-call(f32[8,32,512]{2,1,0:T(8,128)S(1)} %copy-done, ...), custom_call_target="tpu_custom_call", output_to_operand_aliasing={{0}: (12, {}), {1}: (13, {}), {2}: (14, {}), {3}: (15, {}),... | custom-call | tf_op jit(solution)/shard_map/row_edges/pallas_call | solution.py:763
  15.1 0.0 collective-permute-done.2.refs_9_
  15.2 0.1 collective-permute-done.3.refs_10_
  15.3 2.1 %column_edges.1 = (f32[8,32,512]{2,1,0:T(8,128)}, f32[8,32,512]{2,1,0:T(8,128)}, f32[8,32,512]{2,1,0:T(8,128)}, f32[8,32,512]{2,1,0:T(8,128)}, f32[8,32,512]{2,1,0:T(8,128)}) custom-call(f32[8,32,512]{2,1,0:T(8,128)S(1)} %get-tuple-element.39.refs_0_, ...), custom_call_target="tpu_custom_call", output_to_operand_aliasing={{0}: (11, {}), {1}: (12, {}), {2}: (13, {}), {3}: (14, {}),... | custom-call | tf_op jit(solution)/shard_map/column_edges/pallas_call | solution.py:775
  (10 shorter events, 0.0 us)
Async XLA Ops:
  0.6 4.7 %copy-start.6 = (s32[3,32,512]{2,1,0:T(8,128)S(1)}, s32[3,32,512]{2,1,0:T(8,128)}, u32[]{:S(2)}) copy-start(s32[3,32,512]{2,1,0:T(8,128)} %refs_6_.7) | copy-start | bytes 589828
  0.6 4.7 %copy-start.5 = (s32[3,32,512]{2,1,0:T(8,128)S(1)}, s32[3,32,512]{2,1,0:T(8,128)}, u32[]{:S(2)}) copy-start(s32[3,32,512]{2,1,0:T(8,128)} %refs_5_.7) | copy-start | bytes 589828
  0.7 4.6 %copy-start.9 = (s32[32,512]{1,0:T(8,128)S(1)}, s32[32,512]{1,0:T(8,128)}, u32[]{:S(2)}) copy-start(s32[32,512]{1,0:T(8,128)} %refs_9_.7) | copy-start | bytes 196612
  0.7 4.6 %copy-start.8 = (f32[32,512]{1,0:T(8,128)S(1)}, f32[32,512]{1,0:T(8,128)}, u32[]{:S(2)}) copy-start(f32[32,512]{1,0:T(8,128)} %refs_8_.7) | copy-start | bytes 196612
  0.7 4.6 %copy-start.7 = (f32[32,512]{1,0:T(8,128)S(1)}, f32[32,512]{1,0:T(8,128)}, u32[]{:S(2)}) copy-start(f32[32,512]{1,0:T(8,128)} %refs_7_.7) | copy-start | bytes 196612
  0.7 4.6 %copy-start.2 = (f32[8,32,512]{2,1,0:T(8,128)S(1)}, f32[8,32,512]{2,1,0:T(8,128)}, u32[]{:S(2)}) copy-start(f32[8,32,512]{2,1,0:T(8,128)} %refs_2_.7) | copy-start | bytes 1572868
  0.7 4.6 %copy-start.1 = (f32[8,32,512]{2,1,0:T(8,128)S(1)}, f32[8,32,512]{2,1,0:T(8,128)}, u32[]{:S(2)}) copy-start(f32[8,32,512]{2,1,0:T(8,128)} %refs_1_.7) | copy-start | bytes 1572868
  0.7 4.6 %copy-start = (f32[8,32,512]{2,1,0:T(8,128)S(1)}, f32[8,32,512]{2,1,0:T(8,128)}, u32[]{:S(2)}) copy-start(f32[8,32,512]{2,1,0:T(8,128)} %refs_0_.7) | copy-start | bytes 1572868
  0.7 4.6 %copy-start.4 = (f32[3,32,512]{2,1,0:T(8,128)S(1)}, f32[3,32,512]{2,1,0:T(8,128)}, u32[]{:S(2)}) copy-start(f32[3,32,512]{2,1,0:T(8,128)} %refs_4_.7) | copy-start | bytes 589828
  0.7 4.6 %copy-start.3 = (f32[3,32,512]{2,1,0:T(8,128)S(1)}, f32[3,32,512]{2,1,0:T(8,128)}, u32[]{:S(2)}) copy-start(f32[3,32,512]{2,1,0:T(8,128)} %refs_3_.7) | copy-start | bytes 589828
  2.2 6.8 %collective-permute-start.1 = (f32[96,512]{1,0:T(8,128)S(1)}, f32[96,512]{1,0:T(8,128)S(1)}, u32[]{:S(2)}, u32[]{:S(2)}) collective-permute-start(f32[96,512]{1,0:T(8,128)S(1)} %pack_far.1.refs_10_), channel_id=1, source_target_pairs={{0,4},{4,0},{8,12},{12,8},{1,2},{2,1},{3,15},{5,6},{6,5},{7,11},{9... | collective-permute-start | bytes 589832 | tf_op jit(solution)/shard_map/ppermute | solution.py:713
  5.5 3.5 %collective-permute-start = (f32[92,512]{1,0:T(8,128)S(1)}, f32[92,512]{1,0:T(8,128)S(1)}, u32[]{:S(2)}, u32[]{:S(2)}) collective-permute-start(f32[92,512]{1,0:T(8,128)S(1)} %pack_near.1), channel_id=1, source_target_pairs={{0,1},{1,0},{2,3},{3,2},{4,5},{5,4},{6,7},{7,6},{8,9},{9,8},{10,11... | collective-permute-start | bytes 565256 | tf_op jit(solution)/shard_map/ppermute | solution.py:722
  9.3 5.9 %collective-permute-start.2 = (f32[40,128]{1,0:T(8,128)S(1)}, f32[40,128]{1,0:T(8,128)S(1)}, u32[]{:S(2)}, u32[]{:S(2)}) collective-permute-start(f32[40,128]{1,0:T(8,128)S(1)} %get-tuple-element.48), channel_id=1, source_target_pairs={{0,4},{4,8},{8,12},{12,0},{1,5},{5,9},{9,13},{13,1},{2,6},{6,10},{... | collective-permute-start | bytes 61448 | tf_op jit(solution)/shard_map/ppermute | solution.py:760
  11.3 4.0 %collective-permute-start.3 = (f32[40,128]{1,0:T(8,128)S(1)}, f32[40,128]{1,0:T(8,128)S(1)}, u32[]{:S(2)}, u32[]{:S(2)}) collective-permute-start(f32[40,128]{1,0:T(8,128)S(1)} %get-tuple-element.49), channel_id=1, source_target_pairs={{0,12},{4,0},{8,4},{12,8},{1,13},{5,1},{9,5},{13,9},{2,14},{6,2},{... | collective-permute-start | bytes 61448 | tf_op jit(solution)/shard_map/ppermute | solution.py:761

commit v4 on v3

--- a/solution.py
+++ b/solution.py
@@ -248,59 +248,73 @@
         target[...] = packed
 
 
-def merge_rows(one, two, own_west, own_east, halo, halo_static, to_west, to_east):
+def received(one, two):
     even, at_top, at_bottom = place()
-    width = one.shape[1]
-    rows = own_west.shape[0]
-    count = halo.shape[0] // 3
-    lane = iota((TILE, LANES), 1)
-    to_west[:rows, :] = own_west[...]
-    to_east[:rows, :] = own_east[...]
 
     def beyond(here):
         north = jnp.where(even, one[here, :], two[here, :])
         south = jnp.where(even, two[here, :], one[here, :])
         return north, jnp.where(at_bottom, 0.0, south)
 
-    def blank(slots, columns=width):
-        return jnp.zeros((slots, columns), jnp.float32)
-
-    plan, ends_at = shared_plan(count)
-    each = width // LANES
-    tiles, ends = [], []
+    return beyond
+
+
+def blank(slots, columns):
+    return jnp.zeros((slots, columns), jnp.float32)
+
+
+def halo_tiles(one, two, count):
+    _, at_top, _ = place()
+    width = one.shape[1]
+    beyond = received(one, two)
+    plan, _ = shared_plan(count)
+    tiles = []
     for sens in range(count):
         north, south = beyond(slice(STATE_ROWS * sens, STATE_ROWS * (sens + 1)))
         third_north = north[7:8] + 0.5 * north[5:6]
         third_south = south[7:8] - 0.5 * south[4:5]
         fold = jnp.where(at_top, north[6:7], 0.0)
-        tiles.append(jnp.concatenate([north[:2], third_north, blank(2), third_south, south[:2]], axis=0))
-        tiles.append(jnp.concatenate([north[2:4], blank(4), south[2:4]], axis=0))
-        tiles.append(jnp.concatenate([north[4:6], blank(1), fold, blank(1), south[4:7]], axis=0))
+        tiles.append(jnp.concatenate([north[:2], third_north, blank(2, width), third_south, south[:2]], axis=0))
+        tiles.append(jnp.concatenate([north[2:4], blank(4, width), south[2:4]], axis=0))
+        tiles.append(jnp.concatenate([north[4:6], blank(1, width), fold, blank(1, width), south[4:7]], axis=0))
+    for key, kind, turned, at, slots in plan:
+        north, south = beyond(slice(at, at + slots))
+        gap = [blank(DEEP - slots, width)] if slots < DEEP else []
+        plain = jnp.concatenate([north] + gap + gap + [south], axis=0)
+        values = [plain]
+        if kind >= 2 and slots < DEEP:
+            fold = ([north[:-1]] if slots > 1 else []) + gap + [north[-1:]] + gap + [south]
+            if kind == 3:
+                fold = [north[1:], blank(1, width), north[:1]] + gap + [south]
+                values.append(jnp.where(at_top, jnp.concatenate(fold, axis=0), plain))
+            else:
+                values = [jnp.where(at_top, jnp.concatenate(fold, axis=0), plain)]
+        tiles += values
+    tiles.append(blank(TILE, width))
+    return tiles
+
+
+def merge_columns(count, one, two, own_west, own_east, to_west, to_east):
+    _, at_top, _ = place()
+    width = one.shape[1]
+    rows = own_west.shape[0]
+    lane = iota((TILE, LANES), 1)
+    to_west[:rows, :] = own_west[...]
+    to_east[:rows, :] = own_east[...]
+    tiles = halo_tiles(
+        *(jnp.concatenate([ref[:, :LANES], ref[:, width - LANES :]], axis=1) for ref in (one, two)), count
+    )
+    beyond = received(one, two)
+    each = width // LANES
+    _, ends_at = shared_plan(count)
+    ends = []
+    for sens in range(count):
         end_north, end_south = beyond(slice(ends_at + sens // each, ends_at + sens // each + 1))
         mine, turned = (slice(number * LANES, (number + 1) * LANES) for number in (sens % each, each - 1 - sens % each))
         end_north = jnp.where(at_top, end_north[:, turned], end_north[:, mine])
         west = [blank(2, LANES), jnp.where(at_top, end_north, 0.0), blank(5, LANES)]
         east = [blank(2, LANES), jnp.where(at_top, 0.0, end_north), blank(2, LANES), end_south[:, mine], blank(2, LANES)]
         ends.append((jnp.concatenate(west, axis=0), jnp.concatenate(east, axis=0)))
-    for key, kind, turned, at, slots in plan:
-        north, south = beyond(slice(at, at + slots))
-        gap = [blank(DEEP - slots)] if slots < DEEP else []
-        plain = jnp.concatenate([north] + gap + gap + [south], axis=0)
-        values = [plain]
-        if kind >= 2 and slots < DEEP:
-            fold = ([north[:-1]] if slots > 1 else []) + gap + [north[-1:]] + gap + [south]
-            if kind == 3:
-                fold = [north[1:], blank(1), north[:1]] + gap + [south]
-                values.append(jnp.where(at_top, jnp.concatenate(fold, axis=0), plain))
-            else:
-                values = [jnp.where(at_top, jnp.concatenate(fold, axis=0), plain)]
-        tiles += values
-    tiles.append(blank(TILE))
-    for field, value in enumerate(tiles):
-        if field < halo.shape[0]:
-            halo[field] = value
-        else:
-            halo_static[field - halo.shape[0]] = value
     packed = [None, None]
     for key, start, columns, field in column_fields(count):
         pieces = lane_tiles(tiles[field])
@@ -494,7 +508,7 @@
     return sides
 
 
-def interior(*refs):
+def interior(march_now, *refs):
     held = dict(zip(NAMES, refs[:10]))
     results = refs[10:15]
     strips, strips_static, to_west, to_east = refs[15:19]
@@ -506,10 +520,15 @@
         name, step = key
         return (held[name][...] if held[name].ndim == 2 else held[name][step]).astype(jnp.float32)
 
+    if not march_now:
+        for number, strip in enumerate(shared_strips([lane_tiles(field(key, 0)) for key in STRIP_KEYS])):
+            strips_static[number] = strip
+        pack_columns(held, to_west, to_east)
+        for kind in range(3):
+            values = [lane_tiles(held[NAMES[kind]][sens]) for sens in range(sens_count)]
+            strips[kind] = jnp.concatenate(state_strips(values), axis=1)
+        return
     coefficients(field, None, moving, fixed)
-    for number, strip in enumerate(shared_strips([lane_tiles(field(key, 0)) for key in STRIP_KEYS])):
-        strips_static[number] = strip
-    pack_columns(held, to_west, to_east)
 
     def each(turn, carry):
         first = turn * PAIR
@@ -524,18 +543,36 @@
         return carry
 
     lax.fori_loop(0, sens_count // PAIR, each, 0)
-    for kind in range(3):
-        values = [lane_tiles(held[NAMES[kind]][sens]) for sens in range(sens_count)]
-        strips[kind] = jnp.concatenate(state_strips(values), axis=1)
+
+
+def waits_for_top():
+    row = lax.axis_index("lat") * lax.axis_size("sub") + lax.axis_index("sub")
+    return (row == lax.axis_size("lat") * lax.axis_size("sub") - 2) & (lax.axis_index("lon") == 0)
+
+
+def near_and_interior(*refs):
+    pack_near(*refs[:12])
+
+    @pl.when(waits_for_top())
+    def _():
+        interior(True, *refs[:10], *refs[12:])
+
+
+def interior_after(*refs):
+    interior(False, *refs[:10], *refs[19:])
+
+    @pl.when(jnp.logical_not(waits_for_top()))
+    def _():
+        interior(True, *refs[:10], *refs[19:])
 
 
 def row_edges(*refs):
     held = dict(zip(NAMES, refs[:10]))
-    halo, halo_static = refs[10:12]
+    one, two = refs[10:12]
     results = refs[17:22]
     outs = refs[22:27]
     strips, strips_static = refs[27:29]
-    moving, fixed, sems = refs[29:32]
+    halo, halo_static, moving, fixed, sems = refs[29:34]
     _, at_top, _ = place()
     sens_count, rows, width = held["adj_h"].shape
     row = iota((TILE, width), 0)
@@ -547,6 +584,11 @@
     ]
     for copy in copies:
         copy.start()
+    for number, value in enumerate(halo_tiles(one, two, sens_count)):
+        if number < 3 * sens_count:
+            halo[number] = value
+        else:
+            halo_static[number - 3 * sens_count] = value
 
     def shifted_halo(value, kind):
         if kind == 1:
@@ -711,16 +753,6 @@
             route += [(device(lon, row), device(lon, row + 1)), (device(lon, row + 1), device(lon, row))]
         route.append((device(lon, total_rows - 1), device(lons - 1 - lon, total_rows - 1)))
     two = lax.ppermute(packed, GRID, route)
-    one = pl.pallas_call(
-        pack_near,
-        in_specs=[in_vmem] * len(args) + [in_hbm],
-        out_specs=in_vmem,
-        out_shape=jax.ShapeDtypeStruct((message_size(count, width), width), jnp.float32),
-        compiler_params=params,
-        name="pack_near",
-    )(*args, packed)
-    one = lax.ppermute(one, "sub", [(core, core ^ 1) for core in range(subs)])
-
 
     def shape(*dims):
         return jax.ShapeDtypeStruct(dims, jnp.float32)
@@ -732,30 +764,39 @@
         ]
 
     state = shape(*adj_h.shape)
-    first = pl.pallas_call(
-        interior,
-        in_specs=[in_vmem] * 10,
-        out_specs=[in_vmem] * 9,
-        out_shape=[state] * 5
+    inner_shapes = (
+        [state] * 5
         + [shape(3, rows, 2 * LANES), shape(len(STRIP_KEYS), rows, 2 * LANES)]
-        + [shape(rows, LANES)] * 2,
+        + [shape(rows, LANES)] * 2
+    )
+    one, *first = pl.pallas_call(
+        near_and_interior,
+        in_specs=[in_vmem] * 10 + [in_hbm],
+        out_specs=[in_vmem] * 10,
+        out_shape=[shape(message_size(count, width), width)] + inner_shapes,
         scratch_shapes=scratch(rows // TILE, width),
         compiler_params=params,
-        name="interior",
-    )(*args)
+        name="near_and_interior",
+    )(*args, packed)
+    one = lax.ppermute(one, "sub", [(core, core ^ 1) for core in range(subs)])
+    first = pl.pallas_call(
+        interior_after,
+        in_specs=[in_vmem] * 19,
+        out_specs=[in_vmem] * 9,
+        out_shape=inner_shapes,
+        input_output_aliases={10 + number: number for number in range(9)},
+        scratch_shapes=scratch(rows // TILE, width),
+        compiler_params=params,
+        name="interior_after",
+    )(*args, *first)
     results, strips, own_columns = first[:5], first[5:7], first[7:]
 
     full_pack = jax.ShapeDtypeStruct((rows + TILE, LANES), jnp.float32)
-    halo, halo_static, to_west, to_east = pl.pallas_call(
-        merge_rows,
-        out_shape=[
-            shape(3 * count, TILE, width),
-            shape(len(TILES), TILE, width),
-            full_pack,
-            full_pack,
-        ],
+    to_west, to_east = pl.pallas_call(
+        functools.partial(merge_columns, count),
+        out_shape=[full_pack] * 2,
         compiler_params=params,
-        name="merge_rows",
+        name="merge_columns",
     )(one, two, *own_columns)
     from_west = lax.ppermute(to_east, "lon", [(lon, (lon + 1) % lons) for lon in range(lons)])
     from_east = lax.ppermute(to_west, "lon", [(lon, (lon - 1) % lons) for lon in range(lons)])
@@ -766,10 +807,15 @@
         out_specs=[in_vmem] * 5 + [in_hbm] * 5 + [in_vmem] * 2,
         out_shape=[state] * 10 + [shape(3, TILE, 2 * LANES), shape(len(TILES), TILE, 2 * LANES)],
         input_output_aliases={12 + number: number for number in range(5)},
-        scratch_shapes=scratch(3, width) + [pltpu.SemaphoreType.DMA((5,))],
+        scratch_shapes=[
+            pltpu.VMEM((3 * count, TILE, width), jnp.float32),
+            pltpu.VMEM((len(TILES), TILE, width), jnp.float32),
+        ]
+        + scratch(3, width)
+        + [pltpu.SemaphoreType.DMA((5,))],
         compiler_params=params,
         name="row_edges",
-    )(*args, halo, halo_static, *results)
+    )(*args, one, two, *results)
     results, outs, halo_strips = second[:5], second[5:10], second[10:]
 
     return pl.pallas_call(

time: 17.6 us -> 17.5 us (level)
  transfers between devices with their start and end apart: 4 -> 4, of which waited for: 1 -> 0; matrix products, arithmetic and copies ran while one was open for 0% -> 0% of each run, Pallas kernels for 30% -> 31%
where the time goes in v4:
time: 17.5 us; the launch traced here: 17.4 us
  Pallas kernels  9.15 us (52%)
  starting transfers between devices  7.32 us (42%)
  between operations  0.84 us (5%)
    pallas_call x1, Pallas kernels, on_device(): pl.pallas_call(interior_after, in_specs=[in_vmem] * 19, out_specs=[in_vme...  3.3 us
    ppermute x1, starting transfers between devices, on_device(): two = lax.ppermute(packed, GRID, route)  3.09 us
    pallas_call x1, Pallas kernels, on_device(): pl.pallas_call(column_edges, in_specs=[in_vmem] * 11 + [in_hbm] * 5, out_...  2.15 us
    ppermute x1, starting transfers between devices, on_device(): lax.ppermute(to_west, 'lon', [(lon, (lon - 1) % lons) for lon in range(lo...  2.09 us
    ppermute x1, starting transfers between devices, on_device(): lax.ppermute(to_east, 'lon', [(lon, (lon + 1) % lons) for lon in range(lo...  2.04 us
    pallas_call x1, Pallas kernels, on_device(): pl.pallas_call(row_edges, in_specs=[in_vmem] * 17, out_specs=[in_vmem] *...  1.9 us
    pallas_call x1, Pallas kernels, on_device(): pl.pallas_call(pack_far, in_specs=[in_hbm] * len(args), out_specs=in_vmem...  1.46 us
  transfers between devices with their start and end apart: 4, of which 0 were waited for; matrix products, arithmetic and copies ran while one was open for 0% of the time, Pallas kernels for 31%

profile of v4, /device:TPU:0, one launch (start us, length us, event | category | flops | bytes accessed | tf_op | source)
XLA Modules:
  0.0 17.4 jit_solution(14174067134381214284)
XLA Ops:
  0.6 0.0 copy-start
  0.6 0.0 copy-start.1
  0.7 0.0 copy-start.2
  0.7 0.0 copy-start.3
  0.7 0.0 copy-start.4
  0.7 0.0 copy-start.5
  0.7 0.0 copy-start.6
  0.7 0.0 copy-start.7
  0.7 0.0 copy-start.8
  0.7 1.5 %pack_far.1.refs_10_ = f32[96,512]{1,0:T(8,128)S(1)} custom-call(f32[8,32,512]{2,1,0:T(8,128)} %refs_0_.7, f32[8,32,512]{2,1,0:T(8,128)} %refs_1_.7, f32[8,32,512]{2,1,0:T(8,128)} %refs_2_.7, f32[3,32,512]{2,1,0:T(8,128)} %refs_3_.7, f32[3,32,512]{2,1,0:T(8,128)} %refs_4_.7, s32[3,32,512]{2,1,0:T(8,128)} %refs_5_.7, s32[3,32,512]{2,1,0:T(8,128)} %refs_6_.7, ...), custom_call_target="tpu_custom_call" | custom-call | tf_op jit(solution)/shard_map/pack_far/pallas_call | solution.py:733
  2.2 3.1 %collective-permute-start.1 = (f32[96,512]{1,0:T(8,128)S(1)}, f32[96,512]{1,0:T(8,128)S(1)}, u32[]{:S(2)}, u32[]{:S(2)}) collective-permute-start(f32[96,512]{1,0:T(8,128)S(1)} %pack_far.1.refs_10_), channel_id=1, source_target_pairs={{0,4},{4,0},{8,12},{12,8},{1,2},{2,1},{3,15},{5,6},{6,5},{7,11},{9... | collective-permute-start | bytes 589832 | tf_op jit(solution)/shard_map/ppermute | solution.py:755
  5.3 0.0 copy-done.2
  5.4 0.2 near_and_interior.1
  5.5 0.1 collective-permute-start
  5.6 3.3 %interior_after.1 = (f32[8,32,512]{2,1,0:T(8,128)S(1)}, f32[8,32,512]{2,1,0:T(8,128)S(1)}, f32[8,32,512]{2,1,0:T(8,128)S(1)}, f32[8,32,512]{2,1,0:T(8,128)S(1)},...) custom-call(f32[8,32,512]{2,1,0:T(8,128)S(1)} %copy-done, ...), custom_call_target="tpu_custom_call", output_to_operand_aliasing={{0}: (10, {}), {1}: (11, {}), {2}: (12, {}), {3}: (13, {}),... | custom-call | tf_op jit(solution)/shard_map/interior_after/pallas_call | solution.py:782
  8.9 0.0 collective-permute-done.refs_10_.one
  8.9 0.0 collective-permute-done.1.refs_11_.two
  9.0 0.2 %merge_columns.1 = (f32[40,128]{1,0:T(8,128)S(1)}, f32[40,128]{1,0:T(8,128)S(1)}) custom-call(f32[92,512]{1,0:T(8,128)S(1)} %collective-permute-done.refs_10_.one, f32[96,512]{1,0:T(8,128)S(1)} %collective-permute-done.1.refs_11_.two, f32[32,128]{1,0:T(8,128)S(1)} %get-tuple-element.62.own_west, f32[32,128]{1,0:T(8,128)S(1)} %get-tuple-element.63.own_east), custom_call_target="tpu_custom_call" | custom-call | tf_op jit(solution)/shard_map/merge_columns/pallas_call | solution.py:795
  9.2 2.0 %collective-permute-start.2 = (f32[40,128]{1,0:T(8,128)S(1)}, f32[40,128]{1,0:T(8,128)S(1)}, u32[]{:S(2)}, u32[]{:S(2)}) collective-permute-start(f32[40,128]{1,0:T(8,128)S(1)} %get-tuple-element.64), channel_id=1, source_target_pairs={{0,4},{4,8},{8,12},{12,0},{1,5},{5,9},{9,13},{13,1},{2,6},{6,10},{... | collective-permute-start | bytes 61448 | tf_op jit(solution)/shard_map/ppermute | solution.py:801
  11.2 2.1 %collective-permute-start.3 = (f32[40,128]{1,0:T(8,128)S(1)}, f32[40,128]{1,0:T(8,128)S(1)}, u32[]{:S(2)}, u32[]{:S(2)}) collective-permute-start(f32[40,128]{1,0:T(8,128)S(1)} %get-tuple-element.65), channel_id=1, source_target_pairs={{0,12},{4,0},{8,4},{12,8},{1,13},{5,1},{9,5},{13,9},{2,14},{6,2},{... | collective-permute-start | bytes 61448 | tf_op jit(solution)/shard_map/ppermute | solution.py:802
  13.3 1.9 %row_edges.1 = (f32[8,32,512]{2,1,0:T(8,128)S(1)}, f32[8,32,512]{2,1,0:T(8,128)S(1)}, f32[8,32,512]{2,1,0:T(8,128)S(1)}, f32[8,32,512]{2,1,0:T(8,128)S(1)}, f32[...) custom-call(f32[8,32,512]{2,1,0:T(8,128)S(1)} %copy-done, ...), custom_call_target="tpu_custom_call", output_to_operand_aliasing={{0}: (12, {}), {1}: (13, {}), {2}: (14, {}), {3}: (15, {}),... | custom-call | tf_op jit(solution)/shard_map/row_edges/pallas_call | solution.py:804
  15.2 0.0 collective-permute-done.2.refs_9_
  15.2 0.0 collective-permute-done.3.refs_10_
  15.2 2.1 %column_edges.1 = (f32[8,32,512]{2,1,0:T(8,128)}, f32[8,32,512]{2,1,0:T(8,128)}, f32[8,32,512]{2,1,0:T(8,128)}, f32[8,32,512]{2,1,0:T(8,128)}, f32[8,32,512]{2,1,0:T(8,128)}) custom-call(f32[8,32,512]{2,1,0:T(8,128)S(1)} %get-tuple-element.53.refs_0_, ...), custom_call_target="tpu_custom_call", output_to_operand_aliasing={{0}: (11, {}), {1}: (12, {}), {2}: (13, {}), {3}: (14, {}),... | custom-call | tf_op jit(solution)/shard_map/column_edges/pallas_call | solution.py:821
  (10 shorter events, 0.0 us)
Async XLA Ops:
  0.6 4.7 %copy-start = (f32[8,32,512]{2,1,0:T(8,128)S(1)}, f32[8,32,512]{2,1,0:T(8,128)}, u32[]{:S(2)}) copy-start(f32[8,32,512]{2,1,0:T(8,128)} %refs_0_.7) | copy-start | bytes 1572868
  0.6 4.7 %copy-start.1 = (f32[8,32,512]{2,1,0:T(8,128)S(1)}, f32[8,32,512]{2,1,0:T(8,128)}, u32[]{:S(2)}) copy-start(f32[8,32,512]{2,1,0:T(8,128)} %refs_1_.7) | copy-start | bytes 1572868
  0.7 4.6 %copy-start.2 = (f32[8,32,512]{2,1,0:T(8,128)S(1)}, f32[8,32,512]{2,1,0:T(8,128)}, u32[]{:S(2)}) copy-start(f32[8,32,512]{2,1,0:T(8,128)} %refs_2_.7) | copy-start | bytes 1572868
  0.7 4.6 %copy-start.3 = (f32[3,32,512]{2,1,0:T(8,128)S(1)}, f32[3,32,512]{2,1,0:T(8,128)}, u32[]{:S(2)}) copy-start(f32[3,32,512]{2,1,0:T(8,128)} %refs_3_.7) | copy-start | bytes 589828
  0.7 4.6 %copy-start.4 = (f32[3,32,512]{2,1,0:T(8,128)S(1)}, f32[3,32,512]{2,1,0:T(8,128)}, u32[]{:S(2)}) copy-start(f32[3,32,512]{2,1,0:T(8,128)} %refs_4_.7) | copy-start | bytes 589828
  0.7 4.6 %copy-start.5 = (s32[3,32,512]{2,1,0:T(8,128)S(1)}, s32[3,32,512]{2,1,0:T(8,128)}, u32[]{:S(2)}) copy-start(s32[3,32,512]{2,1,0:T(8,128)} %refs_5_.7) | copy-start | bytes 589828
  0.7 4.6 %copy-start.6 = (s32[3,32,512]{2,1,0:T(8,128)S(1)}, s32[3,32,512]{2,1,0:T(8,128)}, u32[]{:S(2)}) copy-start(s32[3,32,512]{2,1,0:T(8,128)} %refs_6_.7) | copy-start | bytes 589828
  0.7 4.6 %copy-start.7 = (f32[32,512]{1,0:T(8,128)S(1)}, f32[32,512]{1,0:T(8,128)}, u32[]{:S(2)}) copy-start(f32[32,512]{1,0:T(8,128)} %refs_7_.7) | copy-start | bytes 196612
  0.7 4.6 %copy-start.8 = (f32[32,512]{1,0:T(8,128)S(1)}, f32[32,512]{1,0:T(8,128)}, u32[]{:S(2)}) copy-start(f32[32,512]{1,0:T(8,128)} %refs_8_.7) | copy-start | bytes 196612
  0.7 4.6 %copy-start.9 = (s32[32,512]{1,0:T(8,128)S(1)}, s32[32,512]{1,0:T(8,128)}, u32[]{:S(2)}) copy-start(s32[32,512]{1,0:T(8,128)} %refs_9_.7) | copy-start | bytes 196612
  2.2 6.8 %collective-permute-start.1 = (f32[96,512]{1,0:T(8,128)S(1)}, f32[96,512]{1,0:T(8,128)S(1)}, u32[]{:S(2)}, u32[]{:S(2)}) collective-permute-start(f32[96,512]{1,0:T(8,128)S(1)} %pack_far.1.refs_10_), channel_id=1, source_target_pairs={{0,4},{4,0},{8,12},{12,8},{1,2},{2,1},{3,15},{5,6},{6,5},{7,11},{9... | collective-permute-start | bytes 589832 | tf_op jit(solution)/shard_map/ppermute | solution.py:755
  5.5 3.4 %collective-permute-start = (f32[92,512]{1,0:T(8,128)S(1)}, f32[92,512]{1,0:T(8,128)S(1)}, u32[]{:S(2)}, u32[]{:S(2)}) collective-permute-start(f32[92,512]{1,0:T(8,128)S(1)} %get-tuple-element.38), channel_id=1, source_target_pairs={{0,1},{1,0},{2,3},{3,2},{4,5},{5,4},{6,7},{7,6},{8,9},{9,8},{10,11... | collective-permute-start | bytes 565256 | tf_op jit(solution)/shard_map/ppermute | solution.py:781
  9.2 6.0 %collective-permute-start.2 = (f32[40,128]{1,0:T(8,128)S(1)}, f32[40,128]{1,0:T(8,128)S(1)}, u32[]{:S(2)}, u32[]{:S(2)}) collective-permute-start(f32[40,128]{1,0:T(8,128)S(1)} %get-tuple-element.64), channel_id=1, source_target_pairs={{0,4},{4,8},{8,12},{12,0},{1,5},{5,9},{9,13},{13,1},{2,6},{6,10},{... | collective-permute-start | bytes 61448 | tf_op jit(solution)/shard_map/ppermute | solution.py:801
  11.2 4.0 %collective-permute-start.3 = (f32[40,128]{1,0:T(8,128)S(1)}, f32[40,128]{1,0:T(8,128)S(1)}, u32[]{:S(2)}, u32[]{:S(2)}) collective-permute-start(f32[40,128]{1,0:T(8,128)S(1)} %get-tuple-element.65), channel_id=1, source_target_pairs={{0,12},{4,0},{8,4},{12,8},{1,13},{5,1},{9,5},{13,9},{2,14},{6,2},{... | collective-permute-start | bytes 61448 | tf_op jit(solution)/shard_map/ppermute | solution.py:802

commit v5 on v4

--- a/solution.py
+++ b/solution.py
@@ -747,12 +747,18 @@
     def device(lon, row):
         return lon * total_rows + row
 
-    route = [(device(lon, 0), device(lon ^ 1, 0)) for lon in range(lons)]
-    for lon in range(lons):
-        for row in range(1, total_rows - 1, 2):
-            route += [(device(lon, row), device(lon, row + 1)), (device(lon, row + 1), device(lon, row))]
-        route.append((device(lon, total_rows - 1), device(lons - 1 - lon, total_rows - 1)))
-    two = lax.ppermute(packed, GRID, route)
+    cases = lax.axis_size("case")
+    each = lons * total_rows
+    route = []
+    for case in range(cases):
+        here = case * each
+        for lon in range(lons):
+            route.append((here + device(lon, 0), (case + 1) % cases * each + device(lon, 0)))
+            for row in range(1, total_rows - 1, 2):
+                low, high = here + device(lon, row), here + device(lon, row + 1)
+                route += [(low, high), (high, low)]
+            route.append((here + device(lon, total_rows - 1), here + device(lons - 1 - lon, total_rows - 1)))
+    two = lax.ppermute(packed, ("case",) + GRID, route)
 
     def shape(*dims):
         return jax.ShapeDtypeStruct(dims, jnp.float32)

time: 17.5 us -> 17.5 us (level)
  no operation moved by 1% of the time
where the time goes in v5:
time: 17.5 us; the launch traced here: 17.4 us
  Pallas kernels  9.15 us (52%)
  starting transfers between devices  7.32 us (42%)
  between operations  0.84 us (5%)
    pallas_call x1, Pallas kernels, on_device(): pl.pallas_call(interior_after, in_specs=[in_vmem] * 19, out_specs=[in_vme...  3.3 us
    ppermute x1, starting transfers between devices, on_device(): two = lax.ppermute(packed, ('case',) + GRID, route)  3.03 us
    pallas_call x1, Pallas kernels, on_device(): pl.pallas_call(column_edges, in_specs=[in_vmem] * 11 + [in_hbm] * 5, out_...  2.15 us
    ppermute x1, starting transfers between devices, on_device(): lax.ppermute(to_west, 'lon', [(lon, (lon - 1) % lons) for lon in range(lo...  2.09 us
    ppermute x1, starting transfers between devices, on_device(): lax.ppermute(to_east, 'lon', [(lon, (lon + 1) % lons) for lon in range(lo...  2.04 us
    pallas_call x1, Pallas kernels, on_device(): pl.pallas_call(row_edges, in_specs=[in_vmem] * 17, out_specs=[in_vmem] *...  1.9 us
    pallas_call x1, Pallas kernels, on_device(): pl.pallas_call(pack_far, in_specs=[in_hbm] * len(args), out_specs=in_vmem...  1.46 us
  transfers between devices with their start and end apart: 4, of which 0 were waited for; matrix products, arithmetic and copies ran while one was open for 0% of the time, Pallas kernels for 31%

profile of v5, /device:TPU:0, one launch (start us, length us, event | category | flops | bytes accessed | tf_op | source)
XLA Modules:
  0.0 17.4 jit_solution(4043238307823684603)
XLA Ops:
  0.6 0.0 copy-start
  0.6 0.0 copy-start.1
  0.7 0.0 copy-start.2
  0.7 0.0 copy-start.3
  0.7 0.0 copy-start.4
  0.7 0.0 copy-start.5
  0.7 0.0 copy-start.6
  0.7 0.0 copy-start.7
  0.7 0.0 copy-start.8
  0.7 0.0 copy-start.9
  0.7 1.5 %pack_far.1.refs_10_ = f32[96,512]{1,0:T(8,128)S(1)} custom-call(f32[8,32,512]{2,1,0:T(8,128)} %refs_0_.7, f32[8,32,512]{2,1,0:T(8,128)} %refs_1_.7, f32[8,32,512]{2,1,0:T(8,128)} %refs_2_.7, f32[3,32,512]{2,1,0:T(8,128)} %refs_3_.7, f32[3,32,512]{2,1,0:T(8,128)} %refs_4_.7, s32[3,32,512]{2,1,0:T(8,128)} %refs_5_.7, s32[3,32,512]{2,1,0:T(8,128)} %refs_6_.7, ...), custom_call_target="tpu_custom_call" | custom-call | tf_op jit(solution)/shard_map/pack_far/pallas_call | solution.py:733
  2.2 3.0 %collective-permute-start.1 = (f32[96,512]{1,0:T(8,128)S(1)}, f32[96,512]{1,0:T(8,128)S(1)}, u32[]{:S(2)}, u32[]{:S(2)}) collective-permute-start(f32[96,512]{1,0:T(8,128)S(1)} %pack_far.1.refs_10_), channel_id=1, source_target_pairs={{0,16},{1,2},{2,1},{3,15},{4,20},{5,6},{6,5},{7,11},{8,24},{9,10},... | collective-permute-start | bytes 589832 | tf_op jit(solution)/shard_map/ppermute | solution.py:761
  5.3 0.2 near_and_interior.1
  5.5 0.2 collective-permute-start
  5.6 3.3 %interior_after.1 = (f32[8,32,512]{2,1,0:T(8,128)S(1)}, f32[8,32,512]{2,1,0:T(8,128)S(1)}, f32[8,32,512]{2,1,0:T(8,128)S(1)}, f32[8,32,512]{2,1,0:T(8,128)S(1)},...) custom-call(f32[8,32,512]{2,1,0:T(8,128)S(1)} %copy-done, ...), custom_call_target="tpu_custom_call", output_to_operand_aliasing={{0}: (10, {}), {1}: (11, {}), {2}: (12, {}), {3}: (13, {}),... | custom-call | tf_op jit(solution)/shard_map/interior_after/pallas_call | solution.py:788
  8.9 0.0 collective-permute-done.refs_10_.one
  8.9 0.0 collective-permute-done.1.refs_11_.two
  9.0 0.2 %merge_columns.1 = (f32[40,128]{1,0:T(8,128)S(1)}, f32[40,128]{1,0:T(8,128)S(1)}) custom-call(f32[92,512]{1,0:T(8,128)S(1)} %collective-permute-done.refs_10_.one, f32[96,512]{1,0:T(8,128)S(1)} %collective-permute-done.1.refs_11_.two, f32[32,128]{1,0:T(8,128)S(1)} %get-tuple-element.62.own_west, f32[32,128]{1,0:T(8,128)S(1)} %get-tuple-element.63.own_east), custom_call_target="tpu_custom_call" | custom-call | tf_op jit(solution)/shard_map/merge_columns/pallas_call | solution.py:801
  9.2 2.0 %collective-permute-start.2 = (f32[40,128]{1,0:T(8,128)S(1)}, f32[40,128]{1,0:T(8,128)S(1)}, u32[]{:S(2)}, u32[]{:S(2)}) collective-permute-start(f32[40,128]{1,0:T(8,128)S(1)} %get-tuple-element.64), channel_id=1, source_target_pairs={{0,4},{4,8},{8,12},{12,0},{1,5},{5,9},{9,13},{13,1},{2,6},{6,10},{... | collective-permute-start | bytes 61448 | tf_op jit(solution)/shard_map/ppermute | solution.py:807
  11.2 2.1 %collective-permute-start.3 = (f32[40,128]{1,0:T(8,128)S(1)}, f32[40,128]{1,0:T(8,128)S(1)}, u32[]{:S(2)}, u32[]{:S(2)}) collective-permute-start(f32[40,128]{1,0:T(8,128)S(1)} %get-tuple-element.65), channel_id=1, source_target_pairs={{0,12},{4,0},{8,4},{12,8},{1,13},{5,1},{9,5},{13,9},{2,14},{6,2},{... | collective-permute-start | bytes 61448 | tf_op jit(solution)/shard_map/ppermute | solution.py:808
  13.3 1.9 %row_edges.1 = (f32[8,32,512]{2,1,0:T(8,128)S(1)}, f32[8,32,512]{2,1,0:T(8,128)S(1)}, f32[8,32,512]{2,1,0:T(8,128)S(1)}, f32[8,32,512]{2,1,0:T(8,128)S(1)}, f32[...) custom-call(f32[8,32,512]{2,1,0:T(8,128)S(1)} %copy-done, ...), custom_call_target="tpu_custom_call", output_to_operand_aliasing={{0}: (12, {}), {1}: (13, {}), {2}: (14, {}), {3}: (15, {}),... | custom-call | tf_op jit(solution)/shard_map/row_edges/pallas_call | solution.py:810
  15.2 0.0 collective-permute-done.2.refs_9_
  15.2 0.0 collective-permute-done.3.refs_10_
  15.2 2.1 %column_edges.1 = (f32[8,32,512]{2,1,0:T(8,128)}, f32[8,32,512]{2,1,0:T(8,128)}, f32[8,32,512]{2,1,0:T(8,128)}, f32[8,32,512]{2,1,0:T(8,128)}, f32[8,32,512]{2,1,0:T(8,128)}) custom-call(f32[8,32,512]{2,1,0:T(8,128)S(1)} %get-tuple-element.53.refs_0_, ...), custom_call_target="tpu_custom_call", output_to_operand_aliasing={{0}: (11, {}), {1}: (12, {}), {2}: (13, {}), {3}: (14, {}),... | custom-call | tf_op jit(solution)/shard_map/column_edges/pallas_call | solution.py:827
  (10 shorter events, 0.0 us)
Async XLA Ops:
  0.6 4.6 %copy-start = (f32[8,32,512]{2,1,0:T(8,128)S(1)}, f32[8,32,512]{2,1,0:T(8,128)}, u32[]{:S(2)}) copy-start(f32[8,32,512]{2,1,0:T(8,128)} %refs_0_.7) | copy-start | bytes 1572868
  0.6 4.6 %copy-start.1 = (f32[8,32,512]{2,1,0:T(8,128)S(1)}, f32[8,32,512]{2,1,0:T(8,128)}, u32[]{:S(2)}) copy-start(f32[8,32,512]{2,1,0:T(8,128)} %refs_1_.7) | copy-start | bytes 1572868
  0.7 4.6 %copy-start.2 = (f32[8,32,512]{2,1,0:T(8,128)S(1)}, f32[8,32,512]{2,1,0:T(8,128)}, u32[]{:S(2)}) copy-start(f32[8,32,512]{2,1,0:T(8,128)} %refs_2_.7) | copy-start | bytes 1572868
  0.7 4.6 %copy-start.3 = (f32[3,32,512]{2,1,0:T(8,128)S(1)}, f32[3,32,512]{2,1,0:T(8,128)}, u32[]{:S(2)}) copy-start(f32[3,32,512]{2,1,0:T(8,128)} %refs_3_.7) | copy-start | bytes 589828
  0.7 4.6 %copy-start.4 = (f32[3,32,512]{2,1,0:T(8,128)S(1)}, f32[3,32,512]{2,1,0:T(8,128)}, u32[]{:S(2)}) copy-start(f32[3,32,512]{2,1,0:T(8,128)} %refs_4_.7) | copy-start | bytes 589828
  0.7 4.6 %copy-start.5 = (s32[3,32,512]{2,1,0:T(8,128)S(1)}, s32[3,32,512]{2,1,0:T(8,128)}, u32[]{:S(2)}) copy-start(s32[3,32,512]{2,1,0:T(8,128)} %refs_5_.7) | copy-start | bytes 589828
  0.7 4.6 %copy-start.6 = (s32[3,32,512]{2,1,0:T(8,128)S(1)}, s32[3,32,512]{2,1,0:T(8,128)}, u32[]{:S(2)}) copy-start(s32[3,32,512]{2,1,0:T(8,128)} %refs_6_.7) | copy-start | bytes 589828
  0.7 4.6 %copy-start.7 = (f32[32,512]{1,0:T(8,128)S(1)}, f32[32,512]{1,0:T(8,128)}, u32[]{:S(2)}) copy-start(f32[32,512]{1,0:T(8,128)} %refs_7_.7) | copy-start | bytes 196612
  0.7 4.6 %copy-start.8 = (f32[32,512]{1,0:T(8,128)S(1)}, f32[32,512]{1,0:T(8,128)}, u32[]{:S(2)}) copy-start(f32[32,512]{1,0:T(8,128)} %refs_8_.7) | copy-start | bytes 196612
  0.7 4.6 %copy-start.9 = (s32[32,512]{1,0:T(8,128)S(1)}, s32[32,512]{1,0:T(8,128)}, u32[]{:S(2)}) copy-start(s32[32,512]{1,0:T(8,128)} %refs_9_.7) | copy-start | bytes 196612
  2.2 6.8 %collective-permute-start.1 = (f32[96,512]{1,0:T(8,128)S(1)}, f32[96,512]{1,0:T(8,128)S(1)}, u32[]{:S(2)}, u32[]{:S(2)}) collective-permute-start(f32[96,512]{1,0:T(8,128)S(1)} %pack_far.1.refs_10_), channel_id=1, source_target_pairs={{0,16},{1,2},{2,1},{3,15},{4,20},{5,6},{6,5},{7,11},{8,24},{9,10},... | collective-permute-start | bytes 589832 | tf_op jit(solution)/shard_map/ppermute | solution.py:761
  5.5 3.5 %collective-permute-start = (f32[92,512]{1,0:T(8,128)S(1)}, f32[92,512]{1,0:T(8,128)S(1)}, u32[]{:S(2)}, u32[]{:S(2)}) collective-permute-start(f32[92,512]{1,0:T(8,128)S(1)} %get-tuple-element.38), channel_id=1, source_target_pairs={{0,1},{1,0},{2,3},{3,2},{4,5},{5,4},{6,7},{7,6},{8,9},{9,8},{10,11... | collective-permute-start | bytes 565256 | tf_op jit(solution)/shard_map/ppermute | solution.py:787
  9.2 6.0 %collective-permute-start.2 = (f32[40,128]{1,0:T(8,128)S(1)}, f32[40,128]{1,0:T(8,128)S(1)}, u32[]{:S(2)}, u32[]{:S(2)}) collective-permute-start(f32[40,128]{1,0:T(8,128)S(1)} %get-tuple-element.64), channel_id=1, source_target_pairs={{0,4},{4,8},{8,12},{12,0},{1,5},{5,9},{9,13},{13,1},{2,6},{6,10},{... | collective-permute-start | bytes 61448 | tf_op jit(solution)/shard_map/ppermute | solution.py:807
  11.2 4.0 %collective-permute-start.3 = (f32[40,128]{1,0:T(8,128)S(1)}, f32[40,128]{1,0:T(8,128)S(1)}, u32[]{:S(2)}, u32[]{:S(2)}) collective-permute-start(f32[40,128]{1,0:T(8,128)S(1)} %get-tuple-element.65), channel_id=1, source_target_pairs={{0,12},{4,0},{8,4},{12,8},{1,13},{5,1},{9,5},{13,9},{2,14},{6,2},{... | collective-permute-start | bytes 61448 | tf_op jit(solution)/shard_map/ppermute | solution.py:808

commit v6 on v5

--- a/solution.py
+++ b/solution.py
@@ -715,7 +715,7 @@
                     ends.at[side, number], outs[number].at[:, :, pl.ds(first, LANES)], sems.at[side, number]
                 )
             )
-            copies[-1].start()
+            copies[-1].start(priority=side)
     for copy in copies:
         copy.wait()
 

time: 17.5 us -> 17.5 us (level)
  no operation moved by 1% of the time
where the time goes in v6:
time: 17.5 us; the launch traced here: 17.4 us
  Pallas kernels  9.15 us (52%)
  starting transfers between devices  7.32 us (42%)
  between operations  0.84 us (5%)
    pallas_call x1, Pallas kernels, on_device(): pl.pallas_call(interior_after, in_specs=[in_vmem] * 19, out_specs=[in_vme...  3.3 us
    ppermute x1, starting transfers between devices, on_device(): two = lax.ppermute(packed, ('case',) + GRID, route)  3.03 us
    pallas_call x1, Pallas kernels, on_device(): pl.pallas_call(column_edges, in_specs=[in_vmem] * 11 + [in_hbm] * 5, out_...  2.15 us
    ppermute x1, starting transfers between devices, on_device(): lax.ppermute(to_west, 'lon', [(lon, (lon - 1) % lons) for lon in range(lo...  2.09 us
    ppermute x1, starting transfers between devices, on_device(): lax.ppermute(to_east, 'lon', [(lon, (lon + 1) % lons) for lon in range(lo...  2.04 us
    pallas_call x1, Pallas kernels, on_device(): pl.pallas_call(row_edges, in_specs=[in_vmem] * 17, out_specs=[in_vmem] *...  1.9 us
    pallas_call x1, Pallas kernels, on_device(): pl.pallas_call(pack_far, in_specs=[in_hbm] * len(args), out_specs=in_vmem...  1.46 us
  transfers between devices with their start and end apart: 4, of which 0 were waited for; matrix products, arithmetic and copies ran while one was open for 0% of the time, Pallas kernels for 31%

profile of v6, /device:TPU:0, one launch (start us, length us, event | category | flops | bytes accessed | tf_op | source)
XLA Modules:
  0.0 17.4 jit_solution(11600413222794199593)
XLA Ops:
  0.6 0.0 copy-start
  0.6 0.0 copy-start.1
  0.7 0.0 copy-start.2
  0.7 0.0 copy-start.3
  0.7 0.0 copy-start.4
  0.7 0.0 copy-start.5
  0.7 0.0 copy-start.6
  0.7 0.0 copy-start.7
  0.7 0.0 copy-start.8
  0.7 0.0 copy-start.9
  0.7 1.5 %pack_far.1.refs_10_ = f32[96,512]{1,0:T(8,128)S(1)} custom-call(f32[8,32,512]{2,1,0:T(8,128)} %refs_0_.7, f32[8,32,512]{2,1,0:T(8,128)} %refs_1_.7, f32[8,32,512]{2,1,0:T(8,128)} %refs_2_.7, f32[3,32,512]{2,1,0:T(8,128)} %refs_3_.7, f32[3,32,512]{2,1,0:T(8,128)} %refs_4_.7, s32[3,32,512]{2,1,0:T(8,128)} %refs_5_.7, s32[3,32,512]{2,1,0:T(8,128)} %refs_6_.7, ...), custom_call_target="tpu_custom_call" | custom-call | tf_op jit(solution)/shard_map/pack_far/pallas_call | solution.py:733
  2.2 3.0 %collective-permute-start.1 = (f32[96,512]{1,0:T(8,128)S(1)}, f32[96,512]{1,0:T(8,128)S(1)}, u32[]{:S(2)}, u32[]{:S(2)}) collective-permute-start(f32[96,512]{1,0:T(8,128)S(1)} %pack_far.1.refs_10_), channel_id=1, source_target_pairs={{0,16},{1,2},{2,1},{3,15},{4,20},{5,6},{6,5},{7,11},{8,24},{9,10},... | collective-permute-start | bytes 589832 | tf_op jit(solution)/shard_map/ppermute | solution.py:761
  5.3 0.2 near_and_interior.1
  5.5 0.2 collective-permute-start
  5.6 3.3 %interior_after.1 = (f32[8,32,512]{2,1,0:T(8,128)S(1)}, f32[8,32,512]{2,1,0:T(8,128)S(1)}, f32[8,32,512]{2,1,0:T(8,128)S(1)}, f32[8,32,512]{2,1,0:T(8,128)S(1)},...) custom-call(f32[8,32,512]{2,1,0:T(8,128)S(1)} %copy-done, ...), custom_call_target="tpu_custom_call", output_to_operand_aliasing={{0}: (10, {}), {1}: (11, {}), {2}: (12, {}), {3}: (13, {}),... | custom-call | tf_op jit(solution)/shard_map/interior_after/pallas_call | solution.py:788
  8.9 0.0 collective-permute-done.refs_10_.one
  8.9 0.0 collective-permute-done.1.refs_11_.two
  9.0 0.2 %merge_columns.1 = (f32[40,128]{1,0:T(8,128)S(1)}, f32[40,128]{1,0:T(8,128)S(1)}) custom-call(f32[92,512]{1,0:T(8,128)S(1)} %collective-permute-done.refs_10_.one, f32[96,512]{1,0:T(8,128)S(1)} %collective-permute-done.1.refs_11_.two, f32[32,128]{1,0:T(8,128)S(1)} %get-tuple-element.62.own_west, f32[32,128]{1,0:T(8,128)S(1)} %get-tuple-element.63.own_east), custom_call_target="tpu_custom_call" | custom-call | tf_op jit(solution)/shard_map/merge_columns/pallas_call | solution.py:801
  9.2 2.0 %collective-permute-start.2 = (f32[40,128]{1,0:T(8,128)S(1)}, f32[40,128]{1,0:T(8,128)S(1)}, u32[]{:S(2)}, u32[]{:S(2)}) collective-permute-start(f32[40,128]{1,0:T(8,128)S(1)} %get-tuple-element.64), channel_id=1, source_target_pairs={{0,4},{4,8},{8,12},{12,0},{1,5},{5,9},{9,13},{13,1},{2,6},{6,10},{... | collective-permute-start | bytes 61448 | tf_op jit(solution)/shard_map/ppermute | solution.py:807
  11.2 2.1 %collective-permute-start.3 = (f32[40,128]{1,0:T(8,128)S(1)}, f32[40,128]{1,0:T(8,128)S(1)}, u32[]{:S(2)}, u32[]{:S(2)}) collective-permute-start(f32[40,128]{1,0:T(8,128)S(1)} %get-tuple-element.65), channel_id=1, source_target_pairs={{0,12},{4,0},{8,4},{12,8},{1,13},{5,1},{9,5},{13,9},{2,14},{6,2},{... | collective-permute-start | bytes 61448 | tf_op jit(solution)/shard_map/ppermute | solution.py:808
  13.3 1.9 %row_edges.1 = (f32[8,32,512]{2,1,0:T(8,128)S(1)}, f32[8,32,512]{2,1,0:T(8,128)S(1)}, f32[8,32,512]{2,1,0:T(8,128)S(1)}, f32[8,32,512]{2,1,0:T(8,128)S(1)}, f32[...) custom-call(f32[8,32,512]{2,1,0:T(8,128)S(1)} %copy-done, ...), custom_call_target="tpu_custom_call", output_to_operand_aliasing={{0}: (12, {}), {1}: (13, {}), {2}: (14, {}), {3}: (15, {}),... | custom-call | tf_op jit(solution)/shard_map/row_edges/pallas_call | solution.py:810
  15.2 0.0 collective-permute-done.2.refs_9_
  15.2 0.0 collective-permute-done.3.refs_10_
  15.2 2.1 %column_edges.1 = (f32[8,32,512]{2,1,0:T(8,128)}, f32[8,32,512]{2,1,0:T(8,128)}, f32[8,32,512]{2,1,0:T(8,128)}, f32[8,32,512]{2,1,0:T(8,128)}, f32[8,32,512]{2,1,0:T(8,128)}) custom-call(f32[8,32,512]{2,1,0:T(8,128)S(1)} %get-tuple-element.53.refs_0_, ...), custom_call_target="tpu_custom_call", output_to_operand_aliasing={{0}: (11, {}), {1}: (12, {}), {2}: (13, {}), {3}: (14, {}),... | custom-call | tf_op jit(solution)/shard_map/column_edges/pallas_call | solution.py:827
  (10 shorter events, 0.0 us)
Async XLA Ops:
  0.6 4.6 %copy-start = (f32[8,32,512]{2,1,0:T(8,128)S(1)}, f32[8,32,512]{2,1,0:T(8,128)}, u32[]{:S(2)}) copy-start(f32[8,32,512]{2,1,0:T(8,128)} %refs_0_.7) | copy-start | bytes 1572868
  0.6 4.6 %copy-start.1 = (f32[8,32,512]{2,1,0:T(8,128)S(1)}, f32[8,32,512]{2,1,0:T(8,128)}, u32[]{:S(2)}) copy-start(f32[8,32,512]{2,1,0:T(8,128)} %refs_1_.7) | copy-start | bytes 1572868
  0.7 4.6 %copy-start.2 = (f32[8,32,512]{2,1,0:T(8,128)S(1)}, f32[8,32,512]{2,1,0:T(8,128)}, u32[]{:S(2)}) copy-start(f32[8,32,512]{2,1,0:T(8,128)} %refs_2_.7) | copy-start | bytes 1572868
  0.7 4.6 %copy-start.3 = (f32[3,32,512]{2,1,0:T(8,128)S(1)}, f32[3,32,512]{2,1,0:T(8,128)}, u32[]{:S(2)}) copy-start(f32[3,32,512]{2,1,0:T(8,128)} %refs_3_.7) | copy-start | bytes 589828
  0.7 4.6 %copy-start.4 = (f32[3,32,512]{2,1,0:T(8,128)S(1)}, f32[3,32,512]{2,1,0:T(8,128)}, u32[]{:S(2)}) copy-start(f32[3,32,512]{2,1,0:T(8,128)} %refs_4_.7) | copy-start | bytes 589828
  0.7 4.6 %copy-start.5 = (s32[3,32,512]{2,1,0:T(8,128)S(1)}, s32[3,32,512]{2,1,0:T(8,128)}, u32[]{:S(2)}) copy-start(s32[3,32,512]{2,1,0:T(8,128)} %refs_5_.7) | copy-start | bytes 589828
  0.7 4.6 %copy-start.6 = (s32[3,32,512]{2,1,0:T(8,128)S(1)}, s32[3,32,512]{2,1,0:T(8,128)}, u32[]{:S(2)}) copy-start(s32[3,32,512]{2,1,0:T(8,128)} %refs_6_.7) | copy-start | bytes 589828
  0.7 4.6 %copy-start.7 = (f32[32,512]{1,0:T(8,128)S(1)}, f32[32,512]{1,0:T(8,128)}, u32[]{:S(2)}) copy-start(f32[32,512]{1,0:T(8,128)} %refs_7_.7) | copy-start | bytes 196612
  0.7 4.6 %copy-start.8 = (f32[32,512]{1,0:T(8,128)S(1)}, f32[32,512]{1,0:T(8,128)}, u32[]{:S(2)}) copy-start(f32[32,512]{1,0:T(8,128)} %refs_8_.7) | copy-start | bytes 196612
  0.7 4.6 %copy-start.9 = (s32[32,512]{1,0:T(8,128)S(1)}, s32[32,512]{1,0:T(8,128)}, u32[]{:S(2)}) copy-start(s32[32,512]{1,0:T(8,128)} %refs_9_.7) | copy-start | bytes 196612
  2.2 6.8 %collective-permute-start.1 = (f32[96,512]{1,0:T(8,128)S(1)}, f32[96,512]{1,0:T(8,128)S(1)}, u32[]{:S(2)}, u32[]{:S(2)}) collective-permute-start(f32[96,512]{1,0:T(8,128)S(1)} %pack_far.1.refs_10_), channel_id=1, source_target_pairs={{0,16},{1,2},{2,1},{3,15},{4,20},{5,6},{6,5},{7,11},{8,24},{9,10},... | collective-permute-start | bytes 589832 | tf_op jit(solution)/shard_map/ppermute | solution.py:761
  5.5 3.5 %collective-permute-start = (f32[92,512]{1,0:T(8,128)S(1)}, f32[92,512]{1,0:T(8,128)S(1)}, u32[]{:S(2)}, u32[]{:S(2)}) collective-permute-start(f32[92,512]{1,0:T(8,128)S(1)} %get-tuple-element.38), channel_id=1, source_target_pairs={{0,1},{1,0},{2,3},{3,2},{4,5},{5,4},{6,7},{7,6},{8,9},{9,8},{10,11... | collective-permute-start | bytes 565256 | tf_op jit(solution)/shard_map/ppermute | solution.py:787
  9.2 6.0 %collective-permute-start.2 = (f32[40,128]{1,0:T(8,128)S(1)}, f32[40,128]{1,0:T(8,128)S(1)}, u32[]{:S(2)}, u32[]{:S(2)}) collective-permute-start(f32[40,128]{1,0:T(8,128)S(1)} %get-tuple-element.64), channel_id=1, source_target_pairs={{0,4},{4,8},{8,12},{12,0},{1,5},{5,9},{9,13},{13,1},{2,6},{6,10},{... | collective-permute-start | bytes 61448 | tf_op jit(solution)/shard_map/ppermute | solution.py:807
  11.2 4.0 %collective-permute-start.3 = (f32[40,128]{1,0:T(8,128)S(1)}, f32[40,128]{1,0:T(8,128)S(1)}, u32[]{:S(2)}, u32[]{:S(2)}) collective-permute-start(f32[40,128]{1,0:T(8,128)S(1)} %get-tuple-element.65), channel_id=1, source_target_pairs={{0,12},{4,0},{8,4},{12,8},{1,13},{5,1},{9,5},{13,9},{2,14},{6,2},{... | collective-permute-start | bytes 61448 | tf_op jit(solution)/shard_map/ppermute | solution.py:808
